TPU v7x, 512 devices: a whole 4x4x16 slice. The times are simulated.
512 devices in a mesh: ctx: 256 (over z, x, y_lo, core), head: 2 (over y_hi).
Axes of the slice: x: 4, y: 4 (y_hi: 2, y_lo: 2; y = y_hi * 2 + y_lo), z: 16, core: 2. Of those that a mesh axis runs over, the one named last changes fastest.
Arguments:
- q_nope: bfloat16 [65536, 16, 128], P('ctx', 'head'), may hold values from -6 to 6
- q_rope: bfloat16 [65536, 16, 64], P('ctx', 'head'), may hold values from -300 to 300
- c_kv: bfloat16 [65536, 512], P('ctx'), may hold values from -6 to 6
- k_rope: bfloat16 [65536, 64], P('ctx'), may hold values from -6 to 6
- block_pos: int32 [512], replicated, may hold values from 0 to 511, as said below
- w_uk: bfloat16 [16, 128, 512], P('head'), may hold values from -0.5 to 0.5
- w_uv: bfloat16 [16, 512, 128], P('head'), may hold values from -6 to 6
Outputs:
- attn_out: bfloat16 [65536, 16, 128], P('ctx', 'head')
Inputs may be any that keep to these rules, and one draw needn't show every extreme that they name: block_pos is the mirrored-pair order turned by some c: block_pos[2 s] = (s + c) mod 256 and block_pos[2 s + 1] = 511 - block_pos[2 s].
All inputs are finite; a program needn't handle non-finite values.
Results may differ from a plain program's by a relative error of at most 0.0072.
Values may be sent and summed in bfloat16 or wider, within the bound.
No kernel may reach another device: no remote copies, remote signals or barrier semaphores. Data moves between devices by JAX's collectives and lax.ppermute only.
A program may use at most 64 MiB of HBM per device.

v0:
```python
import math

import jax
import jax.numpy as jnp
from jax import lax
from jax.sharding import PartitionSpec as P


def from_behind(array, axis, by):
    length = lax.axis_size(axis)
    return lax.ppermute(array, axis, [(i, (i + by) % length) for i in range(length)])


def per_device(q_nope, q_rope, c_kv, k_rope, block_pos, w_uk, w_uv):
    rows = q_nope.shape[0]
    blk = rows // 2
    lat_width = c_kv.shape[1]
    scale = 1.0 / math.sqrt(q_nope.shape[2] + q_rope.shape[2])
    cycle = lax.axis_size("ctx")
    place = lax.axis_index("ctx")
    span = jnp.arange(blk, dtype=jnp.int32)

    def positions(source):
        pair = lax.dynamic_slice_in_dim(block_pos, 2 * source, 2)
        return (pair[:, None] * blk + span[None, :]).reshape(-1)

    packed = jnp.concatenate([c_kv, k_rope], axis=1).reshape(blk, -1)
    from_lower = from_behind(packed, "ctx", 1)
    from_upper = from_behind(packed, "ctx", -1)
    far_lower = from_behind(from_lower, "ctx", 1)
    far_upper = from_behind(from_upper, "ctx", -1)
    pieces = [packed, from_lower, from_upper, far_lower, far_upper]
    keys = jnp.concatenate([piece.reshape(rows, -1) for piece in pieces], axis=0)
    kpos = jnp.concatenate(
        [positions((place - offset) % cycle) for offset in (0, 1, -1, 2, -2)], axis=0
    )
    qpos = positions(place)
    latent = keys[:, :lat_width]
    rotary = keys[:, lat_width:]
    q_lat = jnp.einsum("thn,hnl->thl", q_nope, w_uk, preferred_element_type=jnp.float32).astype(
        jnp.bfloat16
    )
    score = jnp.einsum("thl,kl->thk", q_lat, latent, preferred_element_type=jnp.float32)
    score = (
        score + jnp.einsum("thr,kr->thk", q_rope, rotary, preferred_element_type=jnp.float32)
    ) * scale
    visible = kpos[None, None, :] <= qpos[:, None, None]
    score = jnp.where(visible, score, -1e30)
    top = jnp.max(score, axis=2, keepdims=True)
    expo = jnp.where(visible, jnp.exp(score - top), 0.0)
    total = jnp.sum(expo, axis=2)
    weights = expo.astype(jnp.bfloat16)
    o_lat = jnp.einsum("thk,kl->thl", weights, latent, preferred_element_type=jnp.float32)
    o_lat = (o_lat / total[:, :, None]).astype(jnp.bfloat16)
    return jnp.einsum("thl,hlv->thv", o_lat, w_uv, preferred_element_type=jnp.float32).astype(
        jnp.bfloat16
    )


def solution(mesh):
    placed = (
        P("ctx", "head", None),
        P("ctx", "head", None),
        P("ctx", None),
        P("ctx", None),
        P(),
        P("head", None, None),
        P("head", None, None),
    )
    return jax.shard_map(
        per_device, mesh=mesh, in_specs=placed, out_specs=P("ctx", "head", None), check_vma=False
    )
```

profile of v0, /device:TPU:16, one launch (start us, length us, event | category | flops | bytes accessed | tf_op | source)
XLA Modules:
  0.0 70.2 jit_solution(3220377500140119900)
XLA Ops:
  0.0 0.0 copy-start
  0.0 1.0 %copy.12 = bf16[256,64]{1,0:T(8,128)(2,1)S(1)} copy(bf16[256,64]{0,1:T(8,128)(2,1)} %param.10) | data formatting | bytes 65536 | tf_op args[3]
  1.0 1.7 %pad_maximum_fusion = (bf16[256,576]{1,0:T(8,128)(2,1)S(1)}, bf16[1280,576]{1,0:T(8,128)(2,1)}) fusion(bf16[256,64]{1,0:T(8,128)(2,1)S(1)} %copy.12, bf16[256,512]{1,0:T(8,128)(2,1)} %param.9), kind=kLoop, calls=%fused_computation.19 | loop fusion | flops 589823 | bytes 917504 | tf_op jit(solution)/shard_map/concatenate | solution.py:27
  2.7 0.2 reshape.92
  3.0 13.8 %collective-permute-start.1 = (bf16[128,1152]{1,0:T(8,128)(2,1)S(1)}, bf16[128,1152]{1,0:T(8,128)(2,1)S(1)}, u32[]{:S(2)}, u32[]{:S(2)}) collective-permute-start(bf16[128,1152]{1,0:T(8,128)(2,1)S(1)} %reshape.92), channel_id=1, source_target_pairs={{0,510},{2,0},{4,2},{6,4},{8,6},{10,8},{12,10},{14,12},{16,14},{18... | collective-permute-start | bytes 884744 | tf_op jit(solution)/shard_map/ppermute | solution.py:11
  16.7 1.9 %collective-permute-start = (bf16[128,1152]{1,0:T(8,128)(2,1)S(1)}, bf16[128,1152]{1,0:T(8,128)(2,1)S(1)}, u32[]{:S(2)}, u32[]{:S(2)}) collective-permute-start(bf16[128,1152]{1,0:T(8,128)(2,1)S(1)} %reshape.92), channel_id=1, source_target_pairs={{0,2},{2,4},{4,6},{6,8},{8,10},{10,12},{12,14},{14,16},{16,18},{18... | collective-permute-start | bytes 884744 | tf_op jit(solution)/shard_map/ppermute | solution.py:11
  18.8 1.0 %dynamic-slice_multiply_fusion = (s32[2]{0:T(128)S(1)}, s32[2]{0:T(128)S(1)}, s32[2]{0:T(128)S(1)}, s32[2]{0:T(128)S(1)}, s32[2]{0:T(128)S(1)}, /*index=5*/s32[2]{0:T(128)S(1)}) fusion(s32[512]{0:T(512)} %param.11, s32[]{:T(128)S(6)} %select_n.58, s32[]{:T(128)S(6)} %select_n.55, s32[]{:T(128)S(6)} %select_n.53, s32[]{:T(128)S(6)} %select_n.51, ...), kind=kLoop, calls=%fused_computation.31 | loop fusion | flops 12 | bytes 120 | tf_op jit(solution)/shard_map/mul | solution.py:25
  19.8 0.1 add_bitcast_fusion
  19.9 0.1 constant_dynamic-update-slice_fusion
  19.9 0.1 constant_dynamic-update-slice_fusion.9
  20.0 0.1 constant_dynamic-update-slice_fusion.8
  20.1 0.1 constant_dynamic-update-slice_fusion.7
  20.1 0.1 constant_dynamic-update-slice_fusion.6
  20.2 8.9 %collective-permute-done = bf16[128,1152]{1,0:T(8,128)(2,1)S(1)} collective-permute-done((bf16[128,1152]{1,0:T(8,128)(2,1)S(1)}, bf16[128,1152]{1,0:T(8,128)(2,1)S(1)}, u32[]{:S(2)}, u32[]{:S(2)}) %collective-permute-start) | collective-permute-done | bytes 294944 | tf_op jit(solution)/shard_map/ppermute | solution.py:11
  29.1 1.9 %collective-permute-start.2 = (bf16[128,1152]{1,0:T(8,128)(2,1)S(1)}, bf16[128,1152]{1,0:T(8,128)(2,1)S(1)}, u32[]{:S(2)}, u32[]{:S(2)}) collective-permute-start(bf16[128,1152]{1,0:T(8,128)(2,1)S(1)} %collective-permute-done), channel_id=1, source_target_pairs={{0,2},{2,4},{4,6},{6,8},{8,10},{10,12},{12,14},{14,16},{16,18},{18... | collective-permute-start | bytes 884744 | tf_op jit(solution)/shard_map/ppermute | solution.py:11
  31.0 0.2 broadcast_compare_fusion
  31.3 0.2 reshape.93
  31.5 0.0 collective-permute-done.1
  31.5 7.9 %collective-permute-start.3 = (bf16[128,1152]{1,0:T(8,128)(2,1)S(1)}, bf16[128,1152]{1,0:T(8,128)(2,1)S(1)}, u32[]{:S(2)}, u32[]{:S(2)}) collective-permute-start(bf16[128,1152]{1,0:T(8,128)(2,1)S(1)} %collective-permute-done.1), channel_id=1, source_target_pairs={{0,510},{2,0},{4,2},{6,4},{8,6},{10,8},{12,10},{14,12},{16,14},{18... | collective-permute-start | bytes 884744 | tf_op jit(solution)/shard_map/ppermute | solution.py:11
  39.4 0.0 copy-start.1
  39.4 0.8 %constant_dynamic-update-slice_fusion.4 = bf16[1280,576]{1,0:T(8,128)(2,1)} fusion(bf16[1280,576]{1,0:T(8,128)(2,1)} %get-tuple-element.6, bf16[256,576]{1,0:T(8,128)(2,1)S(1)} %reshape.93), kind=kLoop, calls=%fused_computation.24 | loop fusion | bytes 622592
  40.2 0.2 reshape.94
  40.4 0.8 %constant_dynamic-update-slice_fusion.3 = bf16[1280,576]{1,0:T(8,128)(2,1)} fusion(bf16[1280,576]{1,0:T(8,128)(2,1)} %constant_dynamic-update-slice_fusion.4, bf16[256,576]{1,0:T(8,128)(2,1)S(1)} %reshape.94), kind=kLoop, calls=%fused_computation.23 | loop fusion | bytes 622592
  41.1 0.2 collective-permute-done.2
  41.3 0.2 reshape.95
  41.6 0.8 %constant_dynamic-update-slice_fusion.2 = bf16[1280,576]{1,0:T(8,128)(2,1)} fusion(bf16[1280,576]{1,0:T(8,128)(2,1)} %constant_dynamic-update-slice_fusion.3, bf16[256,576]{1,0:T(8,128)(2,1)S(1)} %reshape.95), kind=kLoop, calls=%fused_computation.22 | loop fusion | bytes 622592
  42.3 1.3 %collective-permute-done.3 = bf16[128,1152]{1,0:T(8,128)(2,1)S(1)} collective-permute-done((bf16[128,1152]{1,0:T(8,128)(2,1)S(1)}, bf16[128,1152]{1,0:T(8,128)(2,1)S(1)}, u32[]{:S(2)}, u32[]{:S(2)}) %collective-permute-start.3) | collective-permute-done | bytes 294944 | tf_op jit(solution)/shard_map/ppermute | solution.py:11
  43.6 0.2 reshape.96
  43.8 0.8 %constant_dynamic-update-slice_fusion.1 = bf16[1280,576]{1,0:T(8,128)(2,1)} fusion(bf16[1280,576]{1,0:T(8,128)(2,1)} %constant_dynamic-update-slice_fusion.2, bf16[256,576]{1,0:T(8,128)(2,1)S(1)} %reshape.96), kind=kLoop, calls=%fused_computation.21 | loop fusion | bytes 622592 | tf_op jit(solution)/shard_map/concatenate | solution.py:33
  44.6 0.0 copy-done.1
  44.6 0.0 copy-start.3
  44.6 6.6 %fusion.22 = f32[1280,256,8]{0,1,2:T(8,128)} fusion(bf16[256,8,64]{0,2,1:T(8,128)(2,1)S(1)} %copy-done.1, bf16[1280,576]{1,0:T(8,128)(2,1)} %constant_dynamic-update-slice_fusion.1), kind=kOutput, calls=%fused_computation.18 | convolution fusion | flops 335544320 | bytes 11075584 | tf_op jit(solution)/shard_map/thr,kr->thk/dot_general | solution.py:45
  51.2 0.0 copy-done
  51.2 0.0 copy-done.3
  51.2 0.0 copy-start.2
  51.2 11.5 %fusion.23 = (f32[256,8]{0,1:T(8,128)S(1)}, bf16[256,8,1280]{2,0,1:T(8,128)(2,1)}) fusion(pred[256,1280]{1,0:T(8,128)(4,1)S(1)} %broadcast_compare_fusion, f32[1280,256,8]{0,1,2:T(8,128)} %fusion.22, bf16[8,128,512]{2,1,0:T(8,128)(2,1)S(1)} %copy-done, bf16[1280,576]{1,0:T(8,128)(2,1)} %constant_dynamic-update-slice_fusion.1, ...), kind=kOutput, calls=%fused_computation.37 | convolution fusion | flops 2972189952 | bytes 19275776 | tf_op jit(solution)/shard_map/sub | solution.py:50
  62.7 0.0 copy-done.2
  62.7 6.3 %fusion.17 = bf16[256,8,128]{2,0,1:T(8,128)(2,1)S(1)} fusion(bf16[8,512,128]{2,1,0:T(8,128)(2,1)S(1)} %copy-done.2, bf16[256,8,1280]{2,0,1:T(8,128)(2,1)} %get-tuple-element.14, f32[256,8]{0,1:T(8,128)S(1)} %get-tuple-element.13, bf16[1280,576]{1,0:T(8,128)(2,1)} %constant_dynamic-update-slice_fusion.1), kind=kOutput, calls=%fused_computation.14 | convolution fusion | flops 2955149312 | bytes 8134656 | tf_op jit(solution)/shard_map/thl,hlv->thv/dot_general | solution.py:55
  69.0 1.1 %copy.15 = bf16[256,8,128]{2,1,0:T(8,128)(2,1)} copy(bf16[256,8,128]{2,0,1:T(8,128)(2,1)S(1)} %fusion.17) | data formatting | bytes 1048576 | tf_op jit(solution)/shard_map/convert_element_type | solution.py:55
  (1 shorter events, 0.0 us)
Async XLA Ops:
  0.0 51.2 %copy-start = (bf16[8,128,512]{2,1,0:T(8,128)(2,1)S(1)}, bf16[8,128,512]{2,1,0:T(8,128)(2,1)}, u32[]{:S(2)}) copy-start(bf16[8,128,512]{2,1,0:T(8,128)(2,1)} %param.12) | copy-start | bytes 3145732
  3.0 28.5 %collective-permute-start.1 = (bf16[128,1152]{1,0:T(8,128)(2,1)S(1)}, bf16[128,1152]{1,0:T(8,128)(2,1)S(1)}, u32[]{:S(2)}, u32[]{:S(2)}) collective-permute-start(bf16[128,1152]{1,0:T(8,128)(2,1)S(1)} %reshape.92), channel_id=1, source_target_pairs={{0,510},{2,0},{4,2},{6,4},{8,6},{10,8},{12,10},{14,12},{16,14},{18... | collective-permute-start | bytes 884744 | tf_op jit(solution)/shard_map/ppermute | solution.py:11
  16.7 12.4 %collective-permute-start = (bf16[128,1152]{1,0:T(8,128)(2,1)S(1)}, bf16[128,1152]{1,0:T(8,128)(2,1)S(1)}, u32[]{:S(2)}, u32[]{:S(2)}) collective-permute-start(bf16[128,1152]{1,0:T(8,128)(2,1)S(1)} %reshape.92), channel_id=1, source_target_pairs={{0,2},{2,4},{4,6},{6,8},{8,10},{10,12},{12,14},{14,16},{16,18},{18... | collective-permute-start | bytes 884744 | tf_op jit(solution)/shard_map/ppermute | solution.py:11
  29.1 12.2 %collective-permute-start.2 = (bf16[128,1152]{1,0:T(8,128)(2,1)S(1)}, bf16[128,1152]{1,0:T(8,128)(2,1)S(1)}, u32[]{:S(2)}, u32[]{:S(2)}) collective-permute-start(bf16[128,1152]{1,0:T(8,128)(2,1)S(1)} %collective-permute-done), channel_id=1, source_target_pairs={{0,2},{2,4},{4,6},{6,8},{8,10},{10,12},{12,14},{14,16},{16,18},{18... | collective-permute-start | bytes 884744 | tf_op jit(solution)/shard_map/ppermute | solution.py:11
  31.5 12.1 %collective-permute-start.3 = (bf16[128,1152]{1,0:T(8,128)(2,1)S(1)}, bf16[128,1152]{1,0:T(8,128)(2,1)S(1)}, u32[]{:S(2)}, u32[]{:S(2)}) collective-permute-start(bf16[128,1152]{1,0:T(8,128)(2,1)S(1)} %collective-permute-done.1), channel_id=1, source_target_pairs={{0,510},{2,0},{4,2},{6,4},{8,6},{10,8},{12,10},{14,12},{16,14},{18... | collective-permute-start | bytes 884744 | tf_op jit(solution)/shard_map/ppermute | solution.py:11
  39.4 5.2 %copy-start.1 = (bf16[256,8,64]{0,2,1:T(8,128)(2,1)S(1)}, bf16[256,8,64]{0,2,1:T(8,128)(2,1)}, u32[]{:S(2)}) copy-start(bf16[256,8,64]{0,2,1:T(8,128)(2,1)} %param.8) | copy-start | bytes 786436
  44.6 6.6 %copy-start.3 = (bf16[256,8,128]{2,1,0:T(8,128)(2,1)S(1)}, bf16[256,8,128]{2,1,0:T(8,128)(2,1)}, u32[]{:S(2)}) copy-start(bf16[256,8,128]{2,1,0:T(8,128)(2,1)} %param.7) | copy-start | bytes 1572868
  51.2 11.5 %copy-start.2 = (bf16[8,512,128]{2,1,0:T(8,128)(2,1)S(1)}, bf16[8,512,128]{2,1,0:T(8,128)(2,1)}, u32[]{:S(2)}) copy-start(bf16[8,512,128]{2,1,0:T(8,128)(2,1)} %param.13) | copy-start | bytes 3145732
where the time goes:
time: 70.4 us; the launch traced here: 70.2 us
  starting transfers between devices  25.4 us (36%)
  matrix products  24.4 us (35%)
  waiting for transfers between devices  10.4 us (15%)
  local copies, waits for them, and re-layouts  6.25 us (9%)
  other arithmetic  3.43 us (5%)
    ppermute x4, starting transfers between devices, from_behind(): lax.ppermute(array, axis, [(i, (i + by) % length) for i in range(length)])  25.4 us
    sub x1, matrix products, per_device(): expo = jnp.where(visible, jnp.exp(score - top), 0.0)  11.5 us
    ppermute x4, waiting for transfers between devices, from_behind(): lax.ppermute(array, axis, [(i, (i + by) % length) for i in range(length)])  10.4 us
    dot_general x1, matrix products, per_device(): jnp.einsum('thr,kr->thk', q_rope, rotary, preferred_element_type=jnp.floa...  6.58 us
    dot_general x1, matrix products, per_device(): jnp.einsum('thl,hlv->thv', o_lat, w_uv, preferred_element_type=jnp.float32)  6.34 us
    unnamed x12, local copies, waits for them, and re-layouts  3.28 us
    concatenate x1, other arithmetic, per_device(): packed = jnp.concatenate([c_kv, k_rope], axis=1).reshape(blk, -1)  1.75 us
  transfers between devices with their start and end apart: 4, of which 3 were waited for; matrix products, arithmetic and copies ran while one was open for 7% of the time, Pallas kernels for 0%

commit v1 on v0

v1 whole, which is shorter than its diff:
```python
import math
import functools
import jax
import jax.numpy as jnp
from jax import lax
from jax.experimental import pallas as pl
from jax.experimental.pallas import tpu as pltpu
from jax.sharding import PartitionSpec as P

NEG = -1e30
LOG2E = 1.4426950408889634


def blocks_kernel(offsets, mchunk, *refs):
    ns = len(refs) - 15
    pos, qn, qr, wk, wv = refs[:5]
    shards = refs[5:5 + ns]
    out = refs[5 + ns]
    qf, qs, kt, vs, ss, os_, low_l, high_l, of = refs[6 + ns:]
    T, H, N = qn.shape
    B = T // 2
    LATW = wk.shape[2]
    R = qr.shape[1]
    W = qs.shape[2]
    HB = H * B
    c2 = LOG2E / math.sqrt(N + R)
    place = lax.axis_index("ctx")
    nctx = pos.shape[0] // 2

    def a_of(off):
        return pos[2 * lax.rem(place - off + nctx, nctx)]

    mine = a_of(0)
    nl = jnp.int32(0)
    nh = jnp.int32(0)
    for i, off in enumerate(offsets(place)):
        if i == 0:
            low_l[nl] = 0
            high_l[nh] = 0
            high_l[nh + 1] = 1
            nl, nh = nl + 1, nh + 2
        else:
            lt = (a_of(off) < mine).astype(jnp.int32)
            low_l[nl] = 2 * i
            nl = nl + lt
            high_l[nh] = 2 * i
            high_l[nh + 1] = 2 * i + 1
            nh = nh + 2 - lt
    low_l[nl] = 0
    high_l[nh] = 0

    zero_k = jnp.zeros((W - LATW - R, B), jnp.bfloat16)
    for i, sh in enumerate(shards):
        rope = sh[T:, :]
        rope = jnp.concatenate([rope[:, :T], rope[:, T:]], axis=0)
        for b in range(2):
            c = sh[b * B:(b + 1) * B, :]
            vs[2 * i + b] = c
            kt[2 * i + b, :LATW, :] = c.T
            kt[2 * i + b, LATW:LATW + R, :] = rope[:, b * B:(b + 1) * B]
            kt[2 * i + b, LATW + R:, :] = zero_k

    qf[...] = qn[...].astype(jnp.float32).reshape(T * H, N)
    zero_q = jnp.zeros((B, W - LATW - R), jnp.bfloat16)
    for h in range(H):
        q = qf[pl.ds(h, T, stride=H), :].astype(jnp.bfloat16)
        ql = jnp.dot(q, wk[h], preferred_element_type=jnp.float32).astype(jnp.bfloat16)
        qrt = qr[h].T
        for b in range(2):
            rr = slice(h * B, (h + 1) * B)
            qs[b, rr, :LATW] = ql[b * B:(b + 1) * B]
            qs[b, rr, LATW:LATW + R] = qrt[b * B:(b + 1) * B]
            qs[b, rr, LATW + R:] = zero_q

    def process(half, n, lst, nb):
        MC = mchunk
        k_items = []
        v_items = []
        for i in range(n):
            b0, b1 = lst[2 * i], lst[2 * i + 1]
            k_items.append(jnp.concatenate([kt[b0], kt[b1]], axis=1))
            v_items.append(jnp.concatenate([vs[b0], vs[b1]], axis=0))
        even = nb == 2 * n
        for i in range(n):
            s = jnp.dot(qs[half], k_items[i], preferred_element_type=jnp.float32)
            if i == 0:
                t_id = lax.broadcasted_iota(jnp.int32, (HB, B), 0) % B
                k_id = lax.broadcasted_iota(jnp.int32, (HB, B), 1)
                tri = k_id <= t_id
                if half == 0:
                    s = jnp.concatenate([jnp.where(tri, s[:, :B], NEG), s[:, B:]], axis=1)
                else:
                    s = jnp.concatenate([s[:, :B], jnp.where(tri, s[:, B:], NEG)], axis=1)
            if i == n - 1:
                s = jnp.concatenate([s[:, :B], jnp.where(even, s[:, B:], NEG)], axis=1)
            ss[:, i * 2 * B:(i + 1) * 2 * B] = s
        for r in range(HB // MC):
            rr = slice(r * MC, (r + 1) * MC)
            mx = ss[rr, :B]
            for j in range(1, 2 * n):
                mx = jnp.maximum(mx, ss[rr, j * B:(j + 1) * B])
            m = jnp.max(mx, axis=1, keepdims=True)
            ps = []
            l = jnp.zeros((MC, B), jnp.float32)
            for j in range(2 * n):
                p = jnp.exp2((ss[rr, j * B:(j + 1) * B] - m) * c2)
                l = l + p
                ps.append(p.astype(jnp.bfloat16))
            tot = jnp.sum(l, axis=1, keepdims=True)
            o = jnp.dot(jnp.concatenate(ps, axis=1), jnp.concatenate(v_items, axis=0), preferred_element_type=jnp.float32)
            os_[half, rr, :] = (o / tot).astype(jnp.bfloat16)

    for half, lst, nb in ((0, low_l, nl), (1, high_l, nh)):
        items = (nb + 1) // 2
        for n in range(1, 6):
            if half == 0 and n > 3 or half == 1 and n < 3:
                continue
            @pl.when(items == n)
            def _(half=half, n=n, lst=lst, nb=nb):
                process(half, n, lst, nb)

    for h in range(H):
        o = jnp.concatenate([os_[0, h * B:(h + 1) * B, :], os_[1, h * B:(h + 1) * B, :]], axis=0)
        of[pl.ds(h, T, stride=H), :] = jnp.dot(o, wv[h], preferred_element_type=jnp.float32)
    out[...] = of[...].reshape(T, H, N).astype(jnp.bfloat16)


def attend(pos, qn, qrt, wk, wv, shards, offsets, mchunk=256):
    T, H, N = qn.shape
    B = T // 2
    ns = len(shards)
    R = qrt.shape[1]
    W = 640
    vm = pl.BlockSpec(memory_space=pltpu.VMEM)
    return pl.pallas_call(
        functools.partial(blocks_kernel, offsets, mchunk),
        out_shape=jax.ShapeDtypeStruct((T, H, N), jnp.bfloat16),
        in_specs=[pl.BlockSpec(memory_space=pltpu.SMEM)] + [vm] * (4 + ns),
        out_specs=vm,
        scratch_shapes=[
            pltpu.VMEM((T * H, N), jnp.float32),
            pltpu.VMEM((2, H * B, W), jnp.bfloat16),
            pltpu.VMEM((2 * ns, W, B), jnp.bfloat16),
            pltpu.VMEM((2 * ns, B, 512), jnp.bfloat16),
            pltpu.VMEM((H * B, 10 * B), jnp.float32),
            pltpu.VMEM((2, H * B, 512), jnp.bfloat16),
            pltpu.SMEM((16,), jnp.int32),
            pltpu.SMEM((16,), jnp.int32),
            pltpu.VMEM((T * H, N), jnp.float32),
        ],
        compiler_params=pltpu.CompilerParams(vmem_limit_bytes=28 * 1024 * 1024),
        name="attend",
    )(pos, qn, qrt, wk, wv, *shards)


def pack_kernel(c, r, out):
    rows = c.shape[0]
    half = r.shape[0] // 2
    out[:rows, :] = c[...]
    out[rows:, :rows] = r[:half, :]
    out[rows:, rows:] = r[half:, :]


def pack(c_kv, k_rope_t):
    rows, width = c_kv.shape
    vm = pl.BlockSpec(memory_space=pltpu.VMEM)
    return pl.pallas_call(
        pack_kernel,
        out_shape=jax.ShapeDtypeStruct((rows + k_rope_t.shape[0] // 2, width), c_kv.dtype),
        in_specs=[vm, vm],
        out_specs=vm,
        name="pack",
    )(c_kv, k_rope_t)


def pairs(n, heads, source):
    out = []
    for t in range(n):
        s = source(t) % n
        for h in range(heads):
            hs = h if s // 4 == t // 4 else heads - 1 - h
            out.append((s * heads + hs, t * heads + h))
    return out


def per_device(q_nope, q_rope, c_kv, k_rope, block_pos, w_uk, w_uv):
    n, heads = lax.axis_size("ctx"), lax.axis_size("head")
    send = lambda x, source: lax.ppermute(x, ("ctx", "head"), pairs(n, heads, source))
    mine = pack(c_kv, k_rope.T)
    mate = send(mine, lambda t: t ^ 1)
    cross = send(mine, lambda t: t - 1 if t % 2 == 0 else t + 1)
    above = send(mine, lambda t: t + 2)
    below = send(mine, lambda t: t - 2)
    q_rope_t = jnp.transpose(q_rope, (1, 2, 0))

    def offsets(place):
        odd = lax.rem(place, 2)
        return (0, 2 * odd - 1, 1 - 2 * odd, 2, -2)

    return attend(block_pos, q_nope, q_rope_t, w_uk, w_uv, (mine, mate, cross, below, above), offsets)


def solution(mesh):
    placed = (
        P("ctx", "head", None),
        P("ctx", "head", None),
        P("ctx", None),
        P("ctx", None),
        P(),
        P("head", None, None),
        P("head", None, None),
    )
    return jax.shard_map(
        per_device, mesh=mesh, in_specs=placed, out_specs=P("ctx", "head", None), check_vma=False
    )
```

time: 70.4 us -> 46.2 us (0.66)
  the two profiles are of different devices: /device:TPU:16 before, /device:TPU:1 now
where the time goes in v1:
time: 46.2 us; the launch traced here: 45.8 us
  starting transfers between devices  29.6 us (64%)
  Pallas kernels  9.73 us (21%)
  local copies, waits for them, and re-layouts  4.36 us (9%)
  waiting for transfers between devices  2.05 us (4%)
    ppermute x4, starting transfers between devices, per_device(): lax.ppermute(x, ('ctx', 'head'), pairs(n, heads, source))  29.6 us
    pallas_call x1, Pallas kernels, attend(): pl.pallas_call(functools.partial(blocks_kernel, offsets, mchunk), out_sha...  7.99 us
    unnamed x12, local copies, waits for them, and re-layouts  4.36 us
    ppermute x4, waiting for transfers between devices, per_device(): lax.ppermute(x, ('ctx', 'head'), pairs(n, heads, source))  2.05 us
    pallas_call x1, Pallas kernels, pack(): pl.pallas_call(pack_kernel, out_shape=jax.ShapeDtypeStruct((rows + k_rope...  1.74 us
  transfers between devices with their start and end apart: 4, of which 1 were waited for; matrix products, arithmetic and copies ran while one was open for 0% of the time, Pallas kernels for 0%

profile of v1, /device:TPU:1, one launch (start us, length us, event | category | flops | bytes accessed | tf_op | source)
XLA Modules:
  0.0 45.8 jit_solution(16844465899607874611)
XLA Ops:
  0.0 0.0 copy-start.3
  0.0 0.0 copy-start.5
  0.0 1.7 %pack.1.refs_5_ = bf16[288,512]{1,0:T(8,128)(2,1)} custom-call(bf16[256,512]{1,0:T(8,128)(2,1)} %c.1, bf16[64,256]{1,0:T(8,128)(2,1)} %bitcast.3), custom_call_target="tpu_custom_call" | custom-call | tf_op jit(solution)/shard_map/pack/pallas_call | solution.py:167
  1.7 16.6 %collective-permute-start.3 = (bf16[288,512]{1,0:T(8,128)(2,1)}, bf16[288,512]{1,0:T(8,128)(2,1)S(1)}, u32[]{:S(2)}, u32[]{:S(2)}) collective-permute-start(bf16[288,512]{1,0:T(8,128)(2,1)} %pack.1.refs_5_), channel_id=1, source_target_pairs={{4,0},{5,1},{6,2},{7,3},{9,4},{8,5},{11,6},{10,7},{12,8},{13,9},{1... | collective-permute-start | bytes 884744 | tf_op jit(solution)/shard_map/ppermute | solution.py:188
  18.3 1.9 %collective-permute-start.2 = (bf16[288,512]{1,0:T(8,128)(2,1)}, bf16[288,512]{1,0:T(8,128)(2,1)S(1)}, u32[]{:S(2)}, u32[]{:S(2)}) collective-permute-start(bf16[288,512]{1,0:T(8,128)(2,1)} %pack.1.refs_5_), channel_id=1, source_target_pairs={{509,0},{508,1},{511,2},{510,3},{0,4},{1,5},{2,6},{3,7},{5,8},{4,9... | collective-permute-start | bytes 884744 | tf_op jit(solution)/shard_map/ppermute | solution.py:188
  20.3 1.9 %collective-permute-start.1 = (bf16[288,512]{1,0:T(8,128)(2,1)}, bf16[288,512]{1,0:T(8,128)(2,1)S(1)}, u32[]{:S(2)}, u32[]{:S(2)}) collective-permute-start(bf16[288,512]{1,0:T(8,128)(2,1)} %pack.1.refs_5_), channel_id=1, source_target_pairs={{511,0},{510,1},{4,2},{5,3},{2,4},{3,5},{9,6},{8,7},{7,8},{6,9},{1... | collective-permute-start | bytes 884744 | tf_op jit(solution)/shard_map/ppermute | solution.py:188
  22.2 9.2 %collective-permute-start = (bf16[288,512]{1,0:T(8,128)(2,1)}, bf16[288,512]{1,0:T(8,128)(2,1)S(1)}, u32[]{:S(2)}, u32[]{:S(2)}) collective-permute-start(bf16[288,512]{1,0:T(8,128)(2,1)} %pack.1.refs_5_), channel_id=1, source_target_pairs={{2,0},{3,1},{0,2},{1,3},{6,4},{7,5},{4,6},{5,7},{10,8},{11,9},{8,1... | collective-permute-start | bytes 884744 | tf_op jit(solution)/shard_map/ppermute | solution.py:188
  31.4 0.0 collective-permute-done.3.refs_9_
  31.4 2.0 %collective-permute-done.2.refs_8_ = bf16[288,512]{1,0:T(8,128)(2,1)S(1)} collective-permute-done((bf16[288,512]{1,0:T(8,128)(2,1)}, bf16[288,512]{1,0:T(8,128)(2,1)S(1)}, u32[]{:S(2)}, u32[]{:S(2)}) %collective-permute-start.2) | collective-permute-done | bytes 294944 | tf_op jit(solution)/shard_map/ppermute | solution.py:188
  33.4 0.0 collective-permute-done.1.refs_7_
  33.4 0.0 collective-permute-done.refs_6_
  33.4 0.0 copy-done.3
  33.4 0.0 copy-done.5
  33.5 0.0 copy-start
  33.5 1.0 %copy-done = bf16[288,512]{1,0:T(8,128)(2,1)S(1)} copy-done((bf16[288,512]{1,0:T(8,128)(2,1)S(1)}, bf16[288,512]{1,0:T(8,128)(2,1)}, u32[]{:S(2)}) %copy-start) | copy-done | bytes 294936
  34.4 0.0 copy-start.1
  34.4 1.2 %copy-done.1 = bf16[8,128,512]{2,1,0:T(8,128)(2,1)S(1)} copy-done((bf16[8,128,512]{2,1,0:T(8,128)(2,1)S(1)}, bf16[8,128,512]{2,1,0:T(8,128)(2,1)}, u32[]{:S(2)}) %copy-start.1) | copy-done | bytes 1048600
  35.6 0.0 copy-start.2
  35.6 1.2 %copy-done.2 = bf16[8,512,128]{2,1,0:T(8,128)(2,1)S(1)} copy-done((bf16[8,512,128]{2,1,0:T(8,128)(2,1)S(1)}, bf16[8,512,128]{2,1,0:T(8,128)(2,1)}, u32[]{:S(2)}) %copy-start.2) | copy-done | bytes 1048600
  36.9 0.0 copy-start.4
  36.9 0.9 %copy-done.4 = bf16[256,8,64]{0,2,1:T(8,128)(2,1)S(1)} copy-done((bf16[256,8,64]{0,2,1:T(8,128)(2,1)S(1)}, bf16[256,8,64]{0,2,1:T(8,128)(2,1)}, u32[]{:S(2)}) %copy-start.4) | copy-done | bytes 262168
  37.8 8.0 %attend.1 = bf16[256,8,128]{2,1,0:T(8,128)(2,1)} custom-call(s32[512]{0:T(512)S(1)} %copy-done.5, bf16[256,8,128]{2,1,0:T(8,128)(2,1)S(1)} %copy-done.3, bf16[8,64,256]{2,1,0:T(8,128)(2,1)S(1)} %bitcast.2, bf16[8,128,512]{2,1,0:T(8,128)(2,1)S(1)} %copy-done.1, bf16[8,512,128]{2,1,0:T(8,128)(2,1)S(1)} %copy-done.2, bf16[288,512]{1,0:T(8,128)(2,1)S(1)} %copy-done, ...), custom_call_target="tpu_custom_call" | custom-call | tf_op jit(solution)/shard_map/attend/pallas_call | solution.py:135
Async XLA Ops:
  0.0 33.4 %copy-start.3 = (bf16[256,8,128]{2,1,0:T(8,128)(2,1)S(1)}, bf16[256,8,128]{2,1,0:T(8,128)(2,1)}, u32[]{:S(2)}) copy-start(bf16[256,8,128]{2,1,0:T(8,128)(2,1)} %refs_1_.1) | copy-start | bytes 1572868
  0.0 33.4 %copy-start.5 = (s32[512]{0:T(512)S(1)}, s32[512]{0:T(512)}, u32[]{:S(2)}) copy-start(s32[512]{0:T(512)} %refs_0_.1) | copy-start | bytes 6148
  1.7 29.6 %collective-permute-start.3 = (bf16[288,512]{1,0:T(8,128)(2,1)}, bf16[288,512]{1,0:T(8,128)(2,1)S(1)}, u32[]{:S(2)}, u32[]{:S(2)}) collective-permute-start(bf16[288,512]{1,0:T(8,128)(2,1)} %pack.1.refs_5_), channel_id=1, source_target_pairs={{4,0},{5,1},{6,2},{7,3},{9,4},{8,5},{11,6},{10,7},{12,8},{13,9},{1... | collective-permute-start | bytes 884744 | tf_op jit(solution)/shard_map/ppermute | solution.py:188
  18.3 15.1 %collective-permute-start.2 = (bf16[288,512]{1,0:T(8,128)(2,1)}, bf16[288,512]{1,0:T(8,128)(2,1)S(1)}, u32[]{:S(2)}, u32[]{:S(2)}) collective-permute-start(bf16[288,512]{1,0:T(8,128)(2,1)} %pack.1.refs_5_), channel_id=1, source_target_pairs={{509,0},{508,1},{511,2},{510,3},{0,4},{1,5},{2,6},{3,7},{5,8},{4,9... | collective-permute-start | bytes 884744 | tf_op jit(solution)/shard_map/ppermute | solution.py:188
  20.3 13.2 %collective-permute-start.1 = (bf16[288,512]{1,0:T(8,128)(2,1)}, bf16[288,512]{1,0:T(8,128)(2,1)S(1)}, u32[]{:S(2)}, u32[]{:S(2)}) collective-permute-start(bf16[288,512]{1,0:T(8,128)(2,1)} %pack.1.refs_5_), channel_id=1, source_target_pairs={{511,0},{510,1},{4,2},{5,3},{2,4},{3,5},{9,6},{8,7},{7,8},{6,9},{1... | collective-permute-start | bytes 884744 | tf_op jit(solution)/shard_map/ppermute | solution.py:188
  22.2 11.2 %collective-permute-start = (bf16[288,512]{1,0:T(8,128)(2,1)}, bf16[288,512]{1,0:T(8,128)(2,1)S(1)}, u32[]{:S(2)}, u32[]{:S(2)}) collective-permute-start(bf16[288,512]{1,0:T(8,128)(2,1)} %pack.1.refs_5_), channel_id=1, source_target_pairs={{2,0},{3,1},{0,2},{1,3},{6,4},{7,5},{4,6},{5,7},{10,8},{11,9},{8,1... | collective-permute-start | bytes 884744 | tf_op jit(solution)/shard_map/ppermute | solution.py:188
  33.5 1.0 %copy-start = (bf16[288,512]{1,0:T(8,128)(2,1)S(1)}, bf16[288,512]{1,0:T(8,128)(2,1)}, u32[]{:S(2)}) copy-start(bf16[288,512]{1,0:T(8,128)(2,1)} %pack.1.refs_5_) | copy-start | bytes 884740
  34.4 1.2 %copy-start.1 = (bf16[8,128,512]{2,1,0:T(8,128)(2,1)S(1)}, bf16[8,128,512]{2,1,0:T(8,128)(2,1)}, u32[]{:S(2)}) copy-start(bf16[8,128,512]{2,1,0:T(8,128)(2,1)} %refs_3_.1) | copy-start | bytes 3145732
  35.6 1.2 %copy-start.2 = (bf16[8,512,128]{2,1,0:T(8,128)(2,1)S(1)}, bf16[8,512,128]{2,1,0:T(8,128)(2,1)}, u32[]{:S(2)}) copy-start(bf16[8,512,128]{2,1,0:T(8,128)(2,1)} %refs_4_.1) | copy-start | bytes 3145732
  36.9 0.9 %copy-start.4 = (bf16[256,8,64]{0,2,1:T(8,128)(2,1)S(1)}, bf16[256,8,64]{0,2,1:T(8,128)(2,1)}, u32[]{:S(2)}) copy-start(bf16[256,8,64]{0,2,1:T(8,128)(2,1)} %param.8) | copy-start | bytes 786436

commit v2 on v0

v2 whole, which is shorter than its diff:
```python
import functools
import math

import jax
import jax.numpy as jnp
from jax import lax
from jax.experimental import pallas as pl
from jax.experimental.pallas import tpu as pltpu
from jax.sharding import PartitionSpec as P

NEG = -1e30
LOG2E = 1.4426950408889634
CHUNK = 256
AHEAD = 3
MIB = 1024 * 1024
FL = 4e9


def place_now():
    return lax.axis_index("ctx")


def phase_kernel(first, last, offsets, ns, split, when, again, *refs):
    refs = list(refs)
    take = lambda k: [refs.pop(0) for _ in range(k)]
    (pos,) = take(1)
    if first:
        qn_h, qr_h, wk_h = take(3)
    else:
        qs, m_in, l_in, o_in = take(4)
    if last:
        (wv_h,) = take(1)
    shards = [take(2) if i in split else take(1)[0] for i in range(ns)]
    if first and again:
        take(4)
    if last:
        (out_h,) = take(1)
        if first:
            (qs,) = take(1)
    else:
        if first:
            (qs,) = take(1)
        m_out, l_out, o_out = take(3)
        if first and not again:
            (passed,) = take(1)
            passed[...] = shards[0][...]
    kt, vs, low_l, high_l = take(4)
    copies = []
    if first:
        qn, qr, wk, qf, sem_q = take(5)
        copies = [
            pltpu.make_async_copy(qn_h, qn, sem_q.at[0]),
            pltpu.make_async_copy(wk_h, wk, sem_q.at[1]),
            pltpu.make_async_copy(qr_h, qr, sem_q.at[2]),
        ]
    if last:
        wv, os_, of, ob, sem_w, sem_o = take(6)
        copy_w = pltpu.make_async_copy(wv_h, wv, sem_w)
    def run():
        for copy in copies:
            copy.start()
        if last:
            copy_w.start()

        _, HB, W = qs.shape
        B = kt.shape[2]
        LATW = vs.shape[2]
        T = 2 * B
        H = HB // B
        R = 2 * (shards[0].shape[0] - T)
        c2 = LOG2E / math.sqrt(LATW // 4 + R)
        place = place_now()
        nctx = pos.shape[0] // 2

        def a_of(off):
            return pos[2 * lax.rem(place - off + nctx, nctx)]

        mine = a_of(0)
        nl = jnp.int32(0)
        nh = jnp.int32(0)
        for i, off in enumerate(offsets(place)):
            if first and i == 0:
                low_l[nl] = 0
                high_l[nh] = 0
                high_l[nh + 1] = 1
                nl, nh = nl + 1, nh + 2
            else:
                lt = (a_of(off) < mine).astype(jnp.int32)
                low_l[nl] = 2 * i
                nl = nl + lt
                high_l[nh] = 2 * i
                high_l[nh + 1] = 2 * i + 1
                nh = nh + 2 - lt
        low_l[nl] = 0
        high_l[nh] = 0

        zero_k = jnp.zeros((W - LATW - R, B), jnp.bfloat16)
        def ready(i, sh):
            rope = sh[T:, :]
            rope = jnp.concatenate([rope[:, :T], rope[:, T:]], axis=0)
            for b in range(2):
                c = sh[b * B:(b + 1) * B, :]
                vs[2 * i + b] = c
                kt[2 * i + b, :LATW, :] = c.T
                kt[2 * i + b, LATW:LATW + R, :] = rope[:, b * B:(b + 1) * B]
                kt[2 * i + b, LATW + R:, :] = zero_k

        for i, sh in enumerate(shards):
            if i in split:
                for odd in range(2):
                    pl.when(lax.rem(place, 2) == odd)(functools.partial(ready, i, sh[odd]))
            else:
                ready(i, sh)

        if first:
            N = wk.shape[1]
            copies[0].wait()
            qf[...] = qn[...].astype(jnp.float32).reshape(T * H, N)
            zero_q = jnp.zeros((B, W - LATW - R), jnp.bfloat16)
            copies[1].wait()
            copies[2].wait()
            for h in range(H):
                q = qf[pl.ds(h, T, stride=H), :].astype(jnp.bfloat16)
                ql = jnp.dot(q, wk[h], preferred_element_type=jnp.float32).astype(jnp.bfloat16)
                qrt = qr[h].T
                for b in range(2):
                    rr = slice(h * B, (h + 1) * B)
                    qs[b, rr, :LATW] = ql[b * B:(b + 1) * B]
                    qs[b, rr, LATW:LATW + R] = qrt[b * B:(b + 1) * B]
                    qs[b, rr, LATW + R:] = zero_q

        def process(*jobs):
            rows = []
            for half, n, lst, nb in jobs:
                k_items = []
                v_items = []
                for i in range(n):
                    b0, b1 = lst[2 * i], lst[2 * i + 1]
                    k_items.append(jnp.concatenate([kt[b0], kt[b1]], axis=1))
                    v_items.append(jnp.concatenate([vs[b0], vs[b1]], axis=0))
                for r in range(HB // CHUNK):
                    rows.append((half, slice(r * CHUNK, (r + 1) * CHUNK), n, nb, k_items, v_items))

            def scores(half, rr, n, nb, k_items, v_items):
                parts = []
                q = qs[half, rr, :]
                for i in range(n):
                    s = jnp.dot(q, k_items[i], preferred_element_type=jnp.float32)
                    s0, s1 = s[:, :B], s[:, B:]
                    if first and i == 0:
                        t_id = lax.broadcasted_iota(jnp.int32, (CHUNK, B), 0) % B
                        k_id = lax.broadcasted_iota(jnp.int32, (CHUNK, B), 1)
                        if half == 0:
                            s0 = jnp.where(k_id <= t_id, s0, NEG)
                        else:
                            s1 = jnp.where(k_id <= t_id, s1, NEG)
                    if nb is not None and i == n - 1:
                        s1 = jnp.where(nb == 2 * n, s1, NEG)
                    parts += [s0, s1]
                return parts

            def weigh(part, half, rr, n, nb, k_items, v_items):
                if n == 0:
                    return m_in[half, rr, :1], l_in[half, rr, :], o_in[half, rr, :]
                mx = part[0]
                for j in range(1, 2 * n):
                    mx = jnp.maximum(mx, part[j])
                m = jnp.max(mx, axis=1, keepdims=True)
                if first:
                    l = jnp.zeros((CHUNK, B), jnp.float32)
                else:
                    old = m_in[half, rr, :1]
                    m = jnp.maximum(m, old)
                    alpha = jnp.exp2((old - m) * c2)
                    l = l_in[half, rr, :] * alpha
                ps = []
                for j in range(2 * n):
                    p = jnp.exp2((part[j] - m) * c2)
                    l = l + p
                    ps.append(p.astype(jnp.bfloat16))
                o = jnp.dot(
                    jnp.concatenate(ps, axis=1), jnp.concatenate(v_items, axis=0), preferred_element_type=jnp.float32
                )
                if not first:
                    o = o + o_in[half, rr, :] * alpha
                return m, l, o

            def keep(half, rr, m, l, o):
                if last:
                    inv = 1.0 / jnp.sum(l, axis=1, keepdims=True)
                    os_[half, rr, :] = (o * inv).astype(jnp.bfloat16)
                else:
                    m_out[half, rr, :] = jnp.broadcast_to(m, (CHUNK, B))
                    l_out[half, rr, :] = l
                    o_out[half, rr, :] = o

            waiting = [scores(*row) for row in rows[:AHEAD]]
            for r, row in enumerate(rows):
                if r + AHEAD < len(rows):
                    waiting.append(scores(*rows[r + AHEAD]))
                keep(*row[:2], *weigh(waiting[r], *row))
                if last and (r + 1 == len(rows) or rows[r + 1][0] != row[0]):
                    output(row[0])

        def output(half):
            if half == 0:
                copy_w.wait()
            for h in range(H):
                o = os_[half, h * B:(h + 1) * B, :]
                of[pl.ds(half * HB + h, B, stride=H), :] = jnp.dot(o, wv[h], preferred_element_type=jnp.float32)
            rows = slice(half * HB, (half + 1) * HB)
            ob[half * B:(half + 1) * B] = of[rows, :].reshape(B, H, of.shape[1]).astype(jnp.bfloat16)
            out_copy(half).start()

        def out_copy(half):
            return pltpu.make_async_copy(ob.at[pl.ds(half * B, B)], out_h.at[pl.ds(half * B, B)], sem_o.at[half])

        if first:
            counts = [((2 + j) // 2, (2 * ns - j + 1) // 2) for j in range(ns)]
        else:
            counts = [((j + 1) // 2, (2 * ns - j + 1) // 2) for j in range(ns + 1)]
        if len(counts) == 1:
            process((0, counts[0][0], low_l, nl), (1, counts[0][1], high_l, nh))
        elif ns == 4:
            usual = nl == 2
            pl.when(usual)(lambda: process((0, *counts[2][:1], low_l, None), (1, counts[2][1], high_l, None)))
            for half, lst, nb in ((0, low_l, nl), (1, high_l, nh)):
                items = (nb + 1) // 2
                for n in sorted({c[half] for j, c in enumerate(counts) if j != 2}):
                    pl.when((items == n) & (nl != 2))(functools.partial(process, (half, n, lst, nb)))
        else:
            for half, lst, nb in ((0, low_l, nl), (1, high_l, nh)):
                items = (nb + 1) // 2
                for n in sorted({c[half] for c in counts}):
                    pl.when(items == n)(functools.partial(process, (half, n, lst, nb)))
        if last:
            for half in range(2):
                out_copy(half).wait()

    if when is None:
        run()
    else:
        pl.when(when(place_now()))(run)


def phase(first, last, offsets, pos, queries, w_uv, shards, when=None, state=None, limit=14):
    ns = len(shards)
    split = [i for i, sh in enumerate(shards) if isinstance(sh, tuple)]
    shards = [x for sh in shards for x in (sh if isinstance(sh, tuple) else (sh,))]
    T = 256
    B = T // 2
    LATW = shards[0].shape[1]
    R = 2 * (shards[0].shape[0] - T)
    W = -(-(LATW + R) // 128) * 128
    if first:
        qn, qr, wk = queries
        H = qn.shape[1]
    else:
        H = queries[0].shape[1] // B
    HB = H * B
    vm = pl.BlockSpec(memory_space=pltpu.VMEM)
    hbm = pl.BlockSpec(memory_space=pltpu.HBM)
    bf, f32 = jnp.bfloat16, jnp.float32
    in_specs = [pl.BlockSpec(memory_space=pltpu.SMEM)] + ([hbm] * 3 if first else [vm] * 4)
    keep = lambda xs, space: [pltpu.with_memory_space_constraint(x, space) for x in xs]
    args = [pos, *keep(queries, pltpu.HBM if first else pltpu.VMEM)]
    if last:
        in_specs.append(hbm)
        args += keep([w_uv], pltpu.HBM)
    in_specs += [vm] * len(shards)
    args += keep(shards, pltpu.VMEM)
    again = state is not None
    aliases = {}
    if first and not last:
        if again:
            aliases = {len(args) + i: i for i in range(4)}
            in_specs += [vm] * 4
            args += keep(state, pltpu.VMEM)
        else:
            aliases = {}
    q_shape = (2, HB, W)
    if last:
        out_shape = jax.ShapeDtypeStruct((T, H, w_uv.shape[2]), bf)
        out_specs = hbm
        scratch = [pltpu.VMEM(q_shape, bf)] if first else []
    else:
        out_shape = [
            pltpu.VMEM(q_shape, bf),
            pltpu.VMEM((2, HB, B), f32),
            pltpu.VMEM((2, HB, B), f32),
            pltpu.VMEM((2, HB, LATW), f32),
        ]
        if not first:
            out_shape = out_shape[1:]
        elif not again:
            out_shape.append(pltpu.VMEM(shards[0].shape, bf))
        out_specs = [vm] * len(out_shape)
        scratch = []
    scratch += [
        pltpu.VMEM((2 * ns, W, B), bf),
        pltpu.VMEM((2 * ns, B, LATW), bf),
        pltpu.SMEM((16,), jnp.int32),
        pltpu.SMEM((16,), jnp.int32),
    ]
    if first:
        scratch += [
            pltpu.VMEM(qn.shape, bf),
            pltpu.VMEM(qr.shape, bf),
            pltpu.VMEM(wk.shape, bf),
            pltpu.VMEM((T * H, qn.shape[2]), f32),
            pltpu.SemaphoreType.DMA((3,)),
        ]
    if last:
        scratch += [
            pltpu.VMEM(w_uv.shape, bf),
            pltpu.VMEM((2, HB, LATW), bf),
            pltpu.VMEM((T * H, w_uv.shape[2]), f32),
            pltpu.VMEM((T, H, w_uv.shape[2]), bf),
            pltpu.SemaphoreType.DMA,
            pltpu.SemaphoreType.DMA((2,)),
        ]
    made = pl.pallas_call(
        functools.partial(phase_kernel, first, last, offsets, ns, split, when, again),
        out_shape=out_shape,
        in_specs=in_specs,
        out_specs=out_specs,
        scratch_shapes=scratch,
        input_output_aliases=aliases,
        compiler_params=pltpu.CompilerParams(vmem_limit_bytes=limit * MIB),
        cost_estimate=pl.CostEstimate(flops=int(FL * ns), bytes_accessed=4 * MIB, transcendentals=MIB),
        name="first" if first else "last" if last else "middle",
    )(*args)
    return made if first or last else [queries[0], *made]


def pack_kernel(c_h, r_h, out, sem):
    rows = c_h.shape[0]
    half = r_h.shape[0] // 2
    copies = [
        pltpu.make_async_copy(c_h, out.at[pl.ds(0, rows), :], sem.at[0]),
        pltpu.make_async_copy(r_h.at[pl.ds(0, half), :], out.at[pl.ds(rows, half), pl.ds(0, rows)], sem.at[1]),
        pltpu.make_async_copy(r_h.at[pl.ds(half, half), :], out.at[pl.ds(rows, half), pl.ds(rows, rows)], sem.at[2]),
    ]
    for copy in copies:
        copy.start()
    for copy in copies:
        copy.wait()


def pack(c_kv, k_rope_t):
    rows, width = c_kv.shape
    hbm = pl.BlockSpec(memory_space=pltpu.HBM)
    return pl.pallas_call(
        pack_kernel,
        out_shape=pltpu.VMEM((rows + k_rope_t.shape[0] // 2, width), c_kv.dtype),
        in_specs=[hbm, hbm],
        out_specs=pl.BlockSpec(memory_space=pltpu.VMEM),
        scratch_shapes=[pltpu.SemaphoreType.DMA((3,))],
        compiler_params=pltpu.CompilerParams(vmem_limit_bytes=2 * MIB),
        name="pack",
    )(*[pltpu.with_memory_space_constraint(x, pltpu.HBM) for x in (c_kv, k_rope_t)])


def hold_kernel(one, _, out):
    out[...] = one[...]


def hold(one, after):
    vm = pl.BlockSpec(memory_space=pltpu.VMEM)
    return pl.pallas_call(
        hold_kernel,
        out_shape=pltpu.VMEM(one.shape, one.dtype),
        in_specs=[vm, vm],
        out_specs=vm,
        compiler_params=pltpu.CompilerParams(vmem_limit_bytes=2 * MIB),
        name="hold",
    )(*[pltpu.with_memory_space_constraint(x, pltpu.VMEM) for x in (one, after)])


def pairs(n, heads, source):
    out = []
    for t in range(n):
        s = source(t)
        if s is None:
            continue
        s %= n
        for h in range(heads):
            hs = h if s // 4 == t // 4 or abs(s - t) > n // 2 else heads - 1 - h
            out.append((s * heads + hs, t * heads + h))
    return out


def per_device(q_nope, q_rope, c_kv, k_rope, block_pos, w_uk, w_uv):
    n, heads = lax.axis_size("ctx"), lax.axis_size("head")
    send = lambda x, source: lax.ppermute(x, ("ctx", "head"), pairs(n, heads, source))
    mine = pack(c_kv, k_rope.T)
    queries = (q_nope, jnp.transpose(q_rope, (1, 2, 0)), w_uk)
    side = lambda place: 2 * lax.rem(place, 2) - 1
    swap = lambda t: t ^ 1
    near = lambda place: (0,)
    below = send(mine, lambda t: t - 2)
    *state, mine = phase(True, False, near, block_pos, queries, None, [mine], when=lambda p: p < 2)
    above = send(mine, lambda t: t + 2)
    mate = send(mine, swap)
    state = phase(True, False, near, block_pos, queries, None, [mine], when=lambda p: p >= 2, state=state)
    cross_b = send(hold(below, state[1]), lambda t: t + 1 if t % 2 == 0 else None)
    cross_a = send(hold(above, state[1]), lambda t: t - 1 if t % 2 else None)
    return phase(False, True, lambda p: (side(p), 2, -2, -side(p)), block_pos, state, w_uv, [mate, below, above, (cross_b, cross_a)])


def solution(mesh):
    placed = (
        P("ctx", "head", None),
        P("ctx", "head", None),
        P("ctx", None),
        P("ctx", None),
        P(),
        P("head", None, None),
        P("head", None, None),
    )
    return jax.shard_map(
        per_device, mesh=mesh, in_specs=placed, out_specs=P("ctx", "head", None), check_vma=False
    )
```

time: 70.4 us -> 36.9 us (0.52)
  the two profiles are of different devices: /device:TPU:16 before, /device:TPU:1 now
where the time goes in v2:
time: 36.9 us; the launch traced here: 36.6 us
  starting transfers between devices  20.9 us (57%)
  Pallas kernels  12.4 us (34%)
  waiting for transfers between devices  2.42 us (7%)
  local copies, waits for them, and re-layouts  0.68 us (2%)
    ppermute x5, starting transfers between devices, per_device(): lax.ppermute(x, ('ctx', 'head'), pairs(n, heads, source))  20.9 us
    pallas_call x3, Pallas kernels, phase(): pl.pallas_call(functools.partial(phase_kernel, first, last, offsets, ns,...  11.4 us
    ppermute x5, waiting for transfers between devices, per_device(): lax.ppermute(x, ('ctx', 'head'), pairs(n, heads, source))  2.42 us
    pallas_call x1, Pallas kernels, pack(): pl.pallas_call(pack_kernel, out_shape=pltpu.VMEM((rows + k_rope_t.shape[0...  0.98 us
  transfers between devices with their start and end apart: 5, of which 1 were waited for; matrix products, arithmetic and copies ran while one was open for 0% of the time, Pallas kernels for 13%

profile of v2, /device:TPU:1, one launch (start us, length us, event | category | flops | bytes accessed | tf_op | source)
XLA Modules:
  0.0 36.6 jit_solution(3614342403766051888)
XLA Ops:
  0.0 1.0 %pack.1.refs_4_ = bf16[288,512]{1,0:T(8,128)(2,1)S(1)} custom-call(bf16[256,512]{1,0:T(8,128)(2,1)} %c_h.1, bf16[64,256]{1,0:T(8,128)(2,1)} %bitcast.2), custom_call_target="tpu_custom_call" | custom-call | tf_op jit(solution)/shard_map/pack/pallas_call | solution.py:353
  1.0 4.0 %collective-permute-start.1 = (bf16[288,512]{1,0:T(8,128)(2,1)S(1)}, bf16[288,512]{1,0:T(8,128)(2,1)S(1)}, u32[]{:S(2)}, u32[]{:S(2)}) collective-permute-start(bf16[288,512]{1,0:T(8,128)(2,1)S(1)} %pack.1.refs_4_), channel_id=1, source_target_pairs={{508,0},{509,1},{510,2},{511,3},{0,4},{1,5},{2,6},{3,7},{5,8},{4,9... | collective-permute-start | bytes 884744 | tf_op jit(solution)/shard_map/ppermute | solution.py:395
  5.0 0.0 copy-start
  5.0 0.7 %copy-done = s32[512]{0:T(512)S(1)} copy-done((s32[512]{0:T(512)S(1)}, s32[512]{0:T(512)}, u32[]{:S(2)}) %copy-start) | copy-done | bytes 2072
  5.7 0.0 copy-start.1
  5.7 4.2 %first.2 = (bf16[2,1024,640]{2,1,0:T(8,128)(2,1)S(1)}, f32[2,1024,128]{2,1,0:T(8,128)S(1)}, f32[2,1024,128]{2,1,0:T(8,128)S(1)}, f32[2,1024,512]{2,1,0:T(8,128)S(1)}, bf16[288,512]{1,0:T(8,128)(2,1)S(1)}) custom-call(s32[512]{0:T(512)S(1)} %copy-done, bf16[256,8,128]{2,1,0:T(8,128)(2,1)} %refs_1_.3, bf16[8,64,256]{2,1,0:T(8,128)(2,1)} %bitcast.3, ...), custom_call_target="tpu_custom_call" | custom-call | flops 4000000000 | bytes 4194304 | tf_op jit(solution)/shard_map/first/pallas_call | solution.py:322
  9.9 9.5 %collective-permute-start.2 = (bf16[288,512]{1,0:T(8,128)(2,1)S(1)}, bf16[288,512]{1,0:T(8,128)(2,1)S(1)}, u32[]{:S(2)}, u32[]{:S(2)}) collective-permute-start(bf16[288,512]{1,0:T(8,128)(2,1)S(1)} %get-tuple-element.14.refs_4_), channel_id=1, source_target_pairs={{4,0},{5,1},{6,2},{7,3},{9,4},{8,5},{11,6},{10,7},{12,8},{13,9},{1... | collective-permute-start | bytes 884744 | tf_op jit(solution)/shard_map/ppermute | solution.py:395
  19.4 2.9 %collective-permute-start = (bf16[288,512]{1,0:T(8,128)(2,1)S(1)}, bf16[288,512]{1,0:T(8,128)(2,1)S(1)}, u32[]{:S(2)}, u32[]{:S(2)}) collective-permute-start(bf16[288,512]{1,0:T(8,128)(2,1)S(1)} %get-tuple-element.14.refs_4_), channel_id=1, source_target_pairs={{2,0},{3,1},{0,2},{1,3},{6,4},{7,5},{4,6},{5,7},{10,8},{11,9},{8,1... | collective-permute-start | bytes 884744 | tf_op jit(solution)/shard_map/ppermute | solution.py:395
  22.3 0.0 copy-done.1
  22.3 0.6 %first.3 = (bf16[2,1024,640]{2,1,0:T(8,128)(2,1)S(1)}, f32[2,1024,128]{2,1,0:T(8,128)S(1)}, f32[2,1024,128]{2,1,0:T(8,128)S(1)}, f32[2,1024,512]{2,1,0:T(8,128)S(1)}) custom-call(s32[512]{0:T(512)S(1)} %copy-done.1, bf16[256,8,128]{2,1,0:T(8,128)(2,1)} %refs_1_.3, ...), custom_call_target="tpu_custom_call", output_to_operand_aliasing={{0}: (5, {}), {1}: (6, {}), {2}: (7, {}), {3}: (8, {})} | custom-call | flops 4000000000 | bytes 4194304 | tf_op jit(solution)/shard_map/first/pallas_call | solution.py:322
  22.9 0.0 collective-permute-done.1.one.refs_7_
  22.9 3.2 %collective-permute-start.3 = (bf16[288,512]{1,0:T(8,128)(2,1)S(1)}, bf16[288,512]{1,0:T(8,128)(2,1)S(1)}, u32[]{:S(2)}, u32[]{:S(2)}) collective-permute-start(bf16[288,512]{1,0:T(8,128)(2,1)S(1)} %hold.2), channel_id=1, source_target_pairs={{2,0},{3,1},{6,4},{7,5},{10,8},{11,9},{14,12},{15,13},{18,16},{19,... | collective-permute-start | bytes 884744 | tf_op jit(solution)/shard_map/ppermute | solution.py:395
  26.2 0.0 collective-permute-done.2.one.refs_8_
  26.2 1.3 %collective-permute-start.4 = (bf16[288,512]{1,0:T(8,128)(2,1)S(1)}, bf16[288,512]{1,0:T(8,128)(2,1)S(1)}, u32[]{:S(2)}, u32[]{:S(2)}) collective-permute-start(bf16[288,512]{1,0:T(8,128)(2,1)S(1)} %hold.3), channel_id=1, source_target_pairs={{0,2},{1,3},{4,6},{5,7},{8,10},{9,11},{12,14},{13,15},{16,18},{17,... | collective-permute-start | bytes 884744 | tf_op jit(solution)/shard_map/ppermute | solution.py:395
  27.5 0.0 collective-permute-done.refs_6_
  27.5 0.0 collective-permute-done.3.refs_9_
  27.5 2.4 %collective-permute-done.4.refs_10_ = bf16[288,512]{1,0:T(8,128)(2,1)S(1)} collective-permute-done((bf16[288,512]{1,0:T(8,128)(2,1)S(1)}, bf16[288,512]{1,0:T(8,128)(2,1)S(1)}, u32[]{:S(2)}, u32[]{:S(2)}) %collective-permute-start.4) | collective-permute-done | bytes 294944 | tf_op jit(solution)/shard_map/ppermute | solution.py:395
  29.9 6.6 %last.1 = bf16[256,8,128]{2,1,0:T(8,128)(2,1)} custom-call(s32[512]{0:T(512)S(1)} %copy-done.1, bf16[2,1024,640]{2,1,0:T(8,128)(2,1)S(1)} %get-tuple-element.19.refs_1_, f32[2,1024,128]{2,1,0:T(8,128)S(1)} %get-tuple-element.20._.refs_2_, f32[2,1024,128]{2,1,0:T(8,128)S(1)} %get-tuple-element.21.refs_3_, f32[2,1024,512]{2,1,0:T(8,128)S(1)} %get-tuple-element.22.refs_4_, ...), custom_call_target="tpu_custom_call" | custom-call | flops 16000000000 | bytes 4194304 | tf_op jit(solution)/shard_map/last/pallas_call | solution.py:322
  (2 shorter events, 0.0 us)
Async XLA Ops:
  1.0 21.9 %collective-permute-start.1 = (bf16[288,512]{1,0:T(8,128)(2,1)S(1)}, bf16[288,512]{1,0:T(8,128)(2,1)S(1)}, u32[]{:S(2)}, u32[]{:S(2)}) collective-permute-start(bf16[288,512]{1,0:T(8,128)(2,1)S(1)} %pack.1.refs_4_), channel_id=1, source_target_pairs={{508,0},{509,1},{510,2},{511,3},{0,4},{1,5},{2,6},{3,7},{5,8},{4,9... | collective-permute-start | bytes 884744 | tf_op jit(solution)/shard_map/ppermute | solution.py:395
  5.0 0.7 %copy-start = (s32[512]{0:T(512)S(1)}, s32[512]{0:T(512)}, u32[]{:S(2)}) copy-start(s32[512]{0:T(512)} %refs_0_.5) | copy-start | bytes 6148
  5.7 16.5 %copy-start.1 = (s32[512]{0:T(512)S(1)}, s32[512]{0:T(512)}, u32[]{:S(2)}) copy-start(s32[512]{0:T(512)} %refs_0_.5) | copy-start | bytes 6148
  9.9 16.2 %collective-permute-start.2 = (bf16[288,512]{1,0:T(8,128)(2,1)S(1)}, bf16[288,512]{1,0:T(8,128)(2,1)S(1)}, u32[]{:S(2)}, u32[]{:S(2)}) collective-permute-start(bf16[288,512]{1,0:T(8,128)(2,1)S(1)} %get-tuple-element.14.refs_4_), channel_id=1, source_target_pairs={{4,0},{5,1},{6,2},{7,3},{9,4},{8,5},{11,6},{10,7},{12,8},{13,9},{1... | collective-permute-start | bytes 884744 | tf_op jit(solution)/shard_map/ppermute | solution.py:395
  19.4 8.1 %collective-permute-start = (bf16[288,512]{1,0:T(8,128)(2,1)S(1)}, bf16[288,512]{1,0:T(8,128)(2,1)S(1)}, u32[]{:S(2)}, u32[]{:S(2)}) collective-permute-start(bf16[288,512]{1,0:T(8,128)(2,1)S(1)} %get-tuple-element.14.refs_4_), channel_id=1, source_target_pairs={{2,0},{3,1},{0,2},{1,3},{6,4},{7,5},{4,6},{5,7},{10,8},{11,9},{8,1... | collective-permute-start | bytes 884744 | tf_op jit(solution)/shard_map/ppermute | solution.py:395
  22.9 4.6 %collective-permute-start.3 = (bf16[288,512]{1,0:T(8,128)(2,1)S(1)}, bf16[288,512]{1,0:T(8,128)(2,1)S(1)}, u32[]{:S(2)}, u32[]{:S(2)}) collective-permute-start(bf16[288,512]{1,0:T(8,128)(2,1)S(1)} %hold.2), channel_id=1, source_target_pairs={{2,0},{3,1},{6,4},{7,5},{10,8},{11,9},{14,12},{15,13},{18,16},{19,... | collective-permute-start | bytes 884744 | tf_op jit(solution)/shard_map/ppermute | solution.py:395
  26.2 3.7 %collective-permute-start.4 = (bf16[288,512]{1,0:T(8,128)(2,1)S(1)}, bf16[288,512]{1,0:T(8,128)(2,1)S(1)}, u32[]{:S(2)}, u32[]{:S(2)}) collective-permute-start(bf16[288,512]{1,0:T(8,128)(2,1)S(1)} %hold.3), channel_id=1, source_target_pairs={{0,2},{1,3},{4,6},{5,7},{8,10},{9,11},{12,14},{13,15},{16,18},{17,... | collective-permute-start | bytes 884744 | tf_op jit(solution)/shard_map/ppermute | solution.py:395

commit v3 on v2

--- a/solution.py
+++ b/solution.py
@@ -20,7 +20,7 @@
     return lax.axis_index("ctx")
 
 
-def phase_kernel(first, last, offsets, ns, split, when, again, *refs):
+def phase_kernel(first, last, offsets, where, packed, when, again, *refs):
     refs = list(refs)
     take = lambda k: [refs.pop(0) for _ in range(k)]
     (pos,) = take(1)
@@ -30,7 +30,9 @@
         qs, m_in, l_in, o_in = take(4)
     if last:
         (wv_h,) = take(1)
-    shards = [take(2) if i in split else take(1)[0] for i in range(ns)]
+    ns = len(where)
+    arrays = take(1 + max(k for parts in where for k, _ in parts))
+    shards = [[(arrays[k], start) for k, start in parts] for parts in where]
     if first and again:
         take(4)
     if last:
@@ -43,7 +45,7 @@
         m_out, l_out, o_out = take(3)
         if first and not again:
             (passed,) = take(1)
-            passed[...] = shards[0][...]
+            passed[...] = arrays[0][...]
     kt, vs, low_l, high_l = take(4)
     copies = []
     if first:
@@ -67,7 +69,7 @@
         LATW = vs.shape[2]
         T = 2 * B
         H = HB // B
-        R = 2 * (shards[0].shape[0] - T)
+        R = 2 * (packed - T)
         c2 = LOG2E / math.sqrt(LATW // 4 + R)
         place = place_now()
         nctx = pos.shape[0] // 2
@@ -95,22 +97,19 @@
         high_l[nh] = 0
 
         zero_k = jnp.zeros((W - LATW - R, B), jnp.bfloat16)
-        def ready(i, sh):
-            rope = sh[T:, :]
+        for i, parts in enumerate(shards):
+            def rows_of(lo, hi):
+                got = [ref[start + lo:start + hi, :] for ref, start in parts]
+                return functools.reduce(lambda x, y: x + y, got)
+
+            rope = rows_of(T, T + R // 2)
             rope = jnp.concatenate([rope[:, :T], rope[:, T:]], axis=0)
             for b in range(2):
-                c = sh[b * B:(b + 1) * B, :]
+                c = rows_of(b * B, (b + 1) * B)
                 vs[2 * i + b] = c
                 kt[2 * i + b, :LATW, :] = c.T
                 kt[2 * i + b, LATW:LATW + R, :] = rope[:, b * B:(b + 1) * B]
                 kt[2 * i + b, LATW + R:, :] = zero_k
-
-        for i, sh in enumerate(shards):
-            if i in split:
-                for odd in range(2):
-                    pl.when(lax.rem(place, 2) == odd)(functools.partial(ready, i, sh[odd]))
-            else:
-                ready(i, sh)
 
         if first:
             N = wk.shape[1]
@@ -243,14 +242,13 @@
         pl.when(when(place_now()))(run)
 
 
-def phase(first, last, offsets, pos, queries, w_uv, shards, when=None, state=None, limit=14):
-    ns = len(shards)
-    split = [i for i, sh in enumerate(shards) if isinstance(sh, tuple)]
-    shards = [x for sh in shards for x in (sh if isinstance(sh, tuple) else (sh,))]
+def phase(first, last, offsets, pos, queries, w_uv, shards, where, when=None, state=None, limit=14):
+    ns = len(where)
     T = 256
     B = T // 2
     LATW = shards[0].shape[1]
-    R = 2 * (shards[0].shape[0] - T)
+    packed = shards[0].shape[0]
+    R = 2 * (packed - T)
     W = -(-(LATW + R) // 128) * 128
     if first:
         qn, qr, wk = queries
@@ -320,7 +318,7 @@
             pltpu.SemaphoreType.DMA((2,)),
         ]
     made = pl.pallas_call(
-        functools.partial(phase_kernel, first, last, offsets, ns, split, when, again),
+        functools.partial(phase_kernel, first, last, offsets, where, packed, when, again),
         out_shape=out_shape,
         in_specs=in_specs,
         out_specs=out_specs,
@@ -361,20 +359,48 @@
     )(*[pltpu.with_memory_space_constraint(x, pltpu.HBM) for x in (c_kv, k_rope_t)])
 
 
-def hold_kernel(one, _, out):
-    out[...] = one[...]
-
-
-def hold(one, after):
+def join_parity_kernel(own, even, odd, _, out):
+    rows = own.shape[0]
+    out[:rows, :] = own[...]
+    parity = lax.rem(place_now(), 2)
+    for k, array in enumerate((even, odd)):
+
+        @pl.when(parity == k)
+        def _():
+            out[rows:, :] = array[...]
+
+
+def join_parity(after, own, even, odd):
     vm = pl.BlockSpec(memory_space=pltpu.VMEM)
+    rows, width = own.shape
     return pl.pallas_call(
-        hold_kernel,
-        out_shape=pltpu.VMEM(one.shape, one.dtype),
-        in_specs=[vm, vm],
+        join_parity_kernel,
+        out_shape=pltpu.VMEM((2 * rows, width), own.dtype),
+        in_specs=[vm] * 4,
         out_specs=vm,
         compiler_params=pltpu.CompilerParams(vmem_limit_bytes=2 * MIB),
-        name="hold",
-    )(*[pltpu.with_memory_space_constraint(x, pltpu.VMEM) for x in (one, after)])
+        name="join_parity",
+    )(*[pltpu.with_memory_space_constraint(x, pltpu.VMEM) for x in (own, even, odd, after)])
+
+
+def join_kernel(*refs):
+    *arrays, _, out = refs
+    rows = arrays[0].shape[0]
+    for i, array in enumerate(arrays):
+        out[i * rows:(i + 1) * rows, :] = array[...]
+
+
+def join(after, *arrays):
+    vm = pl.BlockSpec(memory_space=pltpu.VMEM)
+    rows, width = arrays[0].shape
+    return pl.pallas_call(
+        join_kernel,
+        out_shape=pltpu.VMEM((len(arrays) * rows, width), arrays[0].dtype),
+        in_specs=[vm] * (1 + len(arrays)),
+        out_specs=vm,
+        compiler_params=pltpu.CompilerParams(vmem_limit_bytes=2 * MIB),
+        name="join",
+    )(*[pltpu.with_memory_space_constraint(x, pltpu.VMEM) for x in (*arrays, after)])
 
 
 def pairs(n, heads, source):
@@ -385,7 +411,7 @@
             continue
         s %= n
         for h in range(heads):
-            hs = h if s // 4 == t // 4 or abs(s - t) > n // 2 else heads - 1 - h
+            hs = h if s // 4 == t // 4 or s // 16 != t // 16 else heads - 1 - h
             out.append((s * heads + hs, t * heads + h))
     return out
 
@@ -394,18 +420,30 @@
     n, heads = lax.axis_size("ctx"), lax.axis_size("head")
     send = lambda x, source: lax.ppermute(x, ("ctx", "head"), pairs(n, heads, source))
     mine = pack(c_kv, k_rope.T)
+    rows = mine.shape[0]
     queries = (q_nope, jnp.transpose(q_rope, (1, 2, 0)), w_uk)
     side = lambda place: 2 * lax.rem(place, 2) - 1
-    swap = lambda t: t ^ 1
     near = lambda place: (0,)
+    own = [[(0, 0)]]
     below = send(mine, lambda t: t - 2)
-    *state, mine = phase(True, False, near, block_pos, queries, None, [mine], when=lambda p: p < 2)
-    above = send(mine, lambda t: t + 2)
-    mate = send(mine, swap)
-    state = phase(True, False, near, block_pos, queries, None, [mine], when=lambda p: p >= 2, state=state)
-    cross_b = send(hold(below, state[1]), lambda t: t + 1 if t % 2 == 0 else None)
-    cross_a = send(hold(above, state[1]), lambda t: t - 1 if t % 2 else None)
-    return phase(False, True, lambda p: (side(p), 2, -2, -side(p)), block_pos, state, w_uv, [mate, below, above, (cross_b, cross_a)])
+    above = send(mine, lambda t: t + 2 if t < n - 4 else None)
+    *state, mine = phase(True, False, near, block_pos, queries, w_uv, [mine], own, when=lambda p: p < 2)
+    turn = send(mine, lambda t: t + 2 if t >= n - 4 else None)
+    state = phase(
+        True, False, near, block_pos, queries, w_uv, [mine], own, when=lambda p: p >= 2, state=state
+    )
+    mate = send(join_parity(state[1], mine, above, below), lambda t: t ^ 1)
+    to_end = send(join(state[1], turn), lambda t: t - 1 if t >= n - 4 and t % 2 else None)
+    return phase(
+        False,
+        True,
+        lambda p: (side(p), 2, -2, -side(p)),
+        block_pos,
+        state,
+        w_uv,
+        [below, above, turn, mate, to_end],
+        [[(3, 0)], [(0, 0)], [(1, 0), (2, 0)], [(3, rows), (4, 0)]],
+    )
 
 
 def solution(mesh):

time: 36.9 us -> 35.3 us (0.957)
  starting transfers between devices: 20.9 us -> 18.6 us
  waiting for transfers between devices: 2.42 us -> 3.04 us
    ppermute x5, starting transfers between devices: 20.9 us -> 18.6 us  [per_device(): lax.ppermute(x, ('ctx', 'head'), pairs(n, heads, source))]
    ppermute x5, waiting for transfers between devices: 2.42 us -> 3.04 us  [per_device(): lax.ppermute(x, ('ctx', 'head'), pairs(n, heads, source))]
  transfers between devices with their start and end apart: 5 -> 5, of which waited for: 1 -> 2; matrix products, arithmetic and copies ran while one was open for 0% -> 0% of each run, Pallas kernels for 13% -> 14%
where the time goes in v3:
time: 35.3 us; the launch traced here: 35 us
  starting transfers between devices  18.6 us (53%)
  Pallas kernels  12.4 us (35%)
  waiting for transfers between devices  3.04 us (9%)
  local copies, waits for them, and re-layouts  0.68 us (2%)
    ppermute x5, starting transfers between devices, per_device(): lax.ppermute(x, ('ctx', 'head'), pairs(n, heads, source))  18.6 us
    pallas_call x3, Pallas kernels, phase(): pl.pallas_call(functools.partial(phase_kernel, first, last, offsets, wher...  11.3 us
    ppermute x5, waiting for transfers between devices, per_device(): lax.ppermute(x, ('ctx', 'head'), pairs(n, heads, source))  3.04 us
    pallas_call x1, Pallas kernels, pack(): pl.pallas_call(pack_kernel, out_shape=pltpu.VMEM((rows + k_rope_t.shape[0...  0.98 us
  transfers between devices with their start and end apart: 5, of which 2 were waited for; matrix products, arithmetic and copies ran while one was open for 0% of the time, Pallas kernels for 14%

profile of v3, /device:TPU:1, one launch (start us, length us, event | category | flops | bytes accessed | tf_op | source)
XLA Modules:
  0.0 35.0 jit_solution(5413113361826766383)
XLA Ops:
  0.0 1.0 %pack.1.refs_4_ = bf16[288,512]{1,0:T(8,128)(2,1)S(1)} custom-call(bf16[256,512]{1,0:T(8,128)(2,1)} %c_h.1, bf16[64,256]{1,0:T(8,128)(2,1)} %bitcast.2), custom_call_target="tpu_custom_call" | custom-call | tf_op jit(solution)/shard_map/pack/pallas_call | solution.py:351
  1.0 4.0 %collective-permute-start = (bf16[288,512]{1,0:T(8,128)(2,1)S(1)}, bf16[288,512]{1,0:T(8,128)(2,1)S(1)}, u32[]{:S(2)}, u32[]{:S(2)}) collective-permute-start(bf16[288,512]{1,0:T(8,128)(2,1)S(1)} %pack.1.refs_4_), channel_id=1, source_target_pairs={{508,0},{509,1},{510,2},{511,3},{0,4},{1,5},{2,6},{3,7},{5,8},{4,9... | collective-permute-start | bytes 884744 | tf_op jit(solution)/shard_map/ppermute | solution.py:421
  5.0 1.3 %collective-permute-start.1 = (bf16[288,512]{1,0:T(8,128)(2,1)S(1)}, bf16[288,512]{1,0:T(8,128)(2,1)S(1)}, u32[]{:S(2)}, u32[]{:S(2)}) collective-permute-start(bf16[288,512]{1,0:T(8,128)(2,1)S(1)} %pack.1.refs_4_), channel_id=1, source_target_pairs={{4,0},{5,1},{6,2},{7,3},{9,4},{8,5},{11,6},{10,7},{12,8},{13,9},{1... | collective-permute-start | bytes 884744 | tf_op jit(solution)/shard_map/ppermute | solution.py:421
  6.3 0.0 copy-start
  6.3 0.7 %copy-done = s32[512]{0:T(512)S(1)} copy-done((s32[512]{0:T(512)S(1)}, s32[512]{0:T(512)}, u32[]{:S(2)}) %copy-start) | copy-done | bytes 2072
  7.0 4.2 %first.2 = (bf16[2,1024,640]{2,1,0:T(8,128)(2,1)S(1)}, f32[2,1024,128]{2,1,0:T(8,128)S(1)}, f32[2,1024,128]{2,1,0:T(8,128)S(1)}, f32[2,1024,512]{2,1,0:T(8,128)S(1)}, bf16[288,512]{1,0:T(8,128)(2,1)S(1)}) custom-call(s32[512]{0:T(512)S(1)} %copy-done, bf16[256,8,128]{2,1,0:T(8,128)(2,1)} %refs_1_.3, bf16[8,64,256]{2,1,0:T(8,128)(2,1)} %bitcast.3, ...), custom_call_target="tpu_custom_call" | custom-call | flops 4000000000 | bytes 4194304 | tf_op jit(solution)/shard_map/first/pallas_call | solution.py:320
  11.2 8.9 %collective-permute-start.2 = (bf16[288,512]{1,0:T(8,128)(2,1)S(1)}, bf16[288,512]{1,0:T(8,128)(2,1)S(1)}, u32[]{:S(2)}, u32[]{:S(2)}) collective-permute-start(bf16[288,512]{1,0:T(8,128)(2,1)S(1)} %get-tuple-element.14.refs_4_.own), channel_id=1, source_target_pairs={{508,504},{509,505},{510,506},{511,507},{0,508},{1,509},{2,510},{3... | collective-permute-start | bytes 884744 | tf_op jit(solution)/shard_map/ppermute | solution.py:421
  20.1 0.6 %first.3 = (bf16[2,1024,640]{2,1,0:T(8,128)(2,1)S(1)}, f32[2,1024,128]{2,1,0:T(8,128)S(1)}, f32[2,1024,128]{2,1,0:T(8,128)S(1)}, f32[2,1024,512]{2,1,0:T(8,128)S(1)}) custom-call(s32[512]{0:T(512)S(1)} %copy-done, bf16[256,8,128]{2,1,0:T(8,128)(2,1)} %refs_1_.3, ...), custom_call_target="tpu_custom_call", output_to_operand_aliasing={{0}: (5, {}), {1}: (6, {}), {2}: (7, {}), {3}: (8, {})} | custom-call | flops 4000000000 | bytes 4194304 | tf_op jit(solution)/shard_map/first/pallas_call | solution.py:320
  20.7 2.2 %collective-permute-done.odd.refs_6_ = bf16[288,512]{1,0:T(8,128)(2,1)S(1)} collective-permute-done((bf16[288,512]{1,0:T(8,128)(2,1)S(1)}, bf16[288,512]{1,0:T(8,128)(2,1)S(1)}, u32[]{:S(2)}, u32[]{:S(2)}) %collective-permute-start) | collective-permute-done | bytes 294944 | tf_op jit(solution)/shard_map/ppermute | solution.py:421
  22.9 0.0 collective-permute-done.1.even.refs_7_
  22.9 3.8 %collective-permute-start.3 = (bf16[576,512]{1,0:T(8,128)(2,1)S(1)}, bf16[576,512]{1,0:T(8,128)(2,1)S(1)}, u32[]{:S(2)}, u32[]{:S(2)}) collective-permute-start(bf16[576,512]{1,0:T(8,128)(2,1)S(1)} %join_parity.1), channel_id=1, source_target_pairs={{2,0},{3,1},{0,2},{1,3},{6,4},{7,5},{4,6},{5,7},{10,8},{11,9},{8,1... | collective-permute-start | bytes 1769480 | tf_op jit(solution)/shard_map/ppermute | solution.py:421
  26.7 0.0 collective-permute-done.2.refs_0_.refs_8_
  26.7 0.7 %collective-permute-start.4 = (bf16[288,512]{1,0:T(8,128)(2,1)S(1)}, bf16[288,512]{1,0:T(8,128)(2,1)S(1)}, u32[]{:S(2)}, u32[]{:S(2)}) collective-permute-start(bf16[288,512]{1,0:T(8,128)(2,1)S(1)} %join.1), channel_id=1, source_target_pairs={{504,506},{505,507},{508,510},{509,511}} | collective-permute-start | bytes 884744 | tf_op jit(solution)/shard_map/ppermute | solution.py:421
  27.4 0.0 collective-permute-done.4.refs_10_
  27.4 0.9 %collective-permute-done.3.refs_9_ = bf16[576,512]{1,0:T(8,128)(2,1)S(1)} collective-permute-done((bf16[576,512]{1,0:T(8,128)(2,1)S(1)}, bf16[576,512]{1,0:T(8,128)(2,1)S(1)}, u32[]{:S(2)}, u32[]{:S(2)}) %collective-permute-start.3) | collective-permute-done | bytes 589856 | tf_op jit(solution)/shard_map/ppermute | solution.py:421
  28.3 6.5 %last.1 = bf16[256,8,128]{2,1,0:T(8,128)(2,1)} custom-call(s32[512]{0:T(512)S(1)} %copy-done, bf16[2,1024,640]{2,1,0:T(8,128)(2,1)S(1)} %get-tuple-element.19.refs_1_, f32[2,1024,128]{2,1,0:T(8,128)S(1)} %get-tuple-element.20._.refs_1_.refs_2_, f32[2,1024,128]{2,1,0:T(8,128)S(1)} %get-tuple-element.21.refs_3_, ...), custom_call_target="tpu_custom_call" | custom-call | flops 16000000000 | bytes 4194304 | tf_op jit(solution)/shard_map/last/pallas_call | solution.py:320
  (2 shorter events, 0.1 us)
Async XLA Ops:
  1.0 21.9 %collective-permute-start = (bf16[288,512]{1,0:T(8,128)(2,1)S(1)}, bf16[288,512]{1,0:T(8,128)(2,1)S(1)}, u32[]{:S(2)}, u32[]{:S(2)}) collective-permute-start(bf16[288,512]{1,0:T(8,128)(2,1)S(1)} %pack.1.refs_4_), channel_id=1, source_target_pairs={{508,0},{509,1},{510,2},{511,3},{0,4},{1,5},{2,6},{3,7},{5,8},{4,9... | collective-permute-start | bytes 884744 | tf_op jit(solution)/shard_map/ppermute | solution.py:421
  5.0 17.8 %collective-permute-start.1 = (bf16[288,512]{1,0:T(8,128)(2,1)S(1)}, bf16[288,512]{1,0:T(8,128)(2,1)S(1)}, u32[]{:S(2)}, u32[]{:S(2)}) collective-permute-start(bf16[288,512]{1,0:T(8,128)(2,1)S(1)} %pack.1.refs_4_), channel_id=1, source_target_pairs={{4,0},{5,1},{6,2},{7,3},{9,4},{8,5},{11,6},{10,7},{12,8},{13,9},{1... | collective-permute-start | bytes 884744 | tf_op jit(solution)/shard_map/ppermute | solution.py:421
  6.3 0.7 %copy-start = (s32[512]{0:T(512)S(1)}, s32[512]{0:T(512)}, u32[]{:S(2)}) copy-start(s32[512]{0:T(512)} %refs_0_.5) | copy-start | bytes 6148
  11.2 15.5 %collective-permute-start.2 = (bf16[288,512]{1,0:T(8,128)(2,1)S(1)}, bf16[288,512]{1,0:T(8,128)(2,1)S(1)}, u32[]{:S(2)}, u32[]{:S(2)}) collective-permute-start(bf16[288,512]{1,0:T(8,128)(2,1)S(1)} %get-tuple-element.14.refs_4_.own), channel_id=1, source_target_pairs={{508,504},{509,505},{510,506},{511,507},{0,508},{1,509},{2,510},{3... | collective-permute-start | bytes 884744 | tf_op jit(solution)/shard_map/ppermute | solution.py:421
  22.9 5.4 %collective-permute-start.3 = (bf16[576,512]{1,0:T(8,128)(2,1)S(1)}, bf16[576,512]{1,0:T(8,128)(2,1)S(1)}, u32[]{:S(2)}, u32[]{:S(2)}) collective-permute-start(bf16[576,512]{1,0:T(8,128)(2,1)S(1)} %join_parity.1), channel_id=1, source_target_pairs={{2,0},{3,1},{0,2},{1,3},{6,4},{7,5},{4,6},{5,7},{10,8},{11,9},{8,1... | collective-permute-start | bytes 1769480 | tf_op jit(solution)/shard_map/ppermute | solution.py:421
  26.7 0.7 %collective-permute-start.4 = (bf16[288,512]{1,0:T(8,128)(2,1)S(1)}, bf16[288,512]{1,0:T(8,128)(2,1)S(1)}, u32[]{:S(2)}, u32[]{:S(2)}) collective-permute-start(bf16[288,512]{1,0:T(8,128)(2,1)S(1)} %join.1), channel_id=1, source_target_pairs={{504,506},{505,507},{508,510},{509,511}} | collective-permute-start | bytes 884744 | tf_op jit(solution)/shard_map/ppermute | solution.py:421

commit v4 on v3

--- a/solution.py
+++ b/solution.py
@@ -11,7 +11,7 @@
 NEG = -1e30
 LOG2E = 1.4426950408889634
 CHUNK = 256
-AHEAD = 3
+AHEAD = 4
 MIB = 1024 * 1024
 FL = 4e9
 
@@ -23,7 +23,8 @@
 def phase_kernel(first, last, offsets, where, packed, when, again, *refs):
     refs = list(refs)
     take = lambda k: [refs.pop(0) for _ in range(k)]
-    (pos,) = take(1)
+    if not first:
+        (pos_h,) = take(1)
     if first:
         qn_h, qr_h, wk_h = take(3)
     else:
@@ -47,6 +48,8 @@
             (passed,) = take(1)
             passed[...] = arrays[0][...]
     kt, vs, low_l, high_l = take(4)
+    if not first:
+        pos, sem_p = take(2)
     copies = []
     if first:
         qn, qr, wk, qf, sem_q = take(5)
@@ -59,6 +62,9 @@
         wv, os_, of, ob, sem_w, sem_o = take(6)
         copy_w = pltpu.make_async_copy(wv_h, wv, sem_w)
     def run():
+        if not first:
+            copy_p = pltpu.make_async_copy(pos_h, pos, sem_p)
+            copy_p.start()
         for copy in copies:
             copy.start()
         if last:
@@ -72,12 +78,29 @@
         R = 2 * (packed - T)
         c2 = LOG2E / math.sqrt(LATW // 4 + R)
         place = place_now()
-        nctx = pos.shape[0] // 2
+
+        zero_k = jnp.zeros((W - LATW - R, B), jnp.bfloat16)
+        for i, parts in enumerate(shards):
+            def rows_of(lo, hi):
+                got = [ref[start + lo:start + hi, :] for ref, start in parts]
+                return functools.reduce(lambda x, y: x + y, got)
+
+            rope = rows_of(T, T + R // 2)
+            rope = jnp.concatenate([rope[:, :T], rope[:, T:]], axis=0)
+            for b in range(2):
+                c = rows_of(b * B, (b + 1) * B)
+                vs[2 * i + b] = c
+                kt[2 * i + b, :LATW, :] = c.T
+                kt[2 * i + b, LATW:LATW + R, :] = rope[:, b * B:(b + 1) * B]
+                kt[2 * i + b, LATW + R:, :] = zero_k
 
         def a_of(off):
+            nctx = pos.shape[0] // 2
             return pos[2 * lax.rem(place - off + nctx, nctx)]
 
-        mine = a_of(0)
+        if not first:
+            copy_p.wait()
+            mine = a_of(0)
         nl = jnp.int32(0)
         nh = jnp.int32(0)
         for i, off in enumerate(offsets(place)):
@@ -95,21 +118,6 @@
                 nh = nh + 2 - lt
         low_l[nl] = 0
         high_l[nh] = 0
-
-        zero_k = jnp.zeros((W - LATW - R, B), jnp.bfloat16)
-        for i, parts in enumerate(shards):
-            def rows_of(lo, hi):
-                got = [ref[start + lo:start + hi, :] for ref, start in parts]
-                return functools.reduce(lambda x, y: x + y, got)
-
-            rope = rows_of(T, T + R // 2)
-            rope = jnp.concatenate([rope[:, :T], rope[:, T:]], axis=0)
-            for b in range(2):
-                c = rows_of(b * B, (b + 1) * B)
-                vs[2 * i + b] = c
-                kt[2 * i + b, :LATW, :] = c.T
-                kt[2 * i + b, LATW:LATW + R, :] = rope[:, b * B:(b + 1) * B]
-                kt[2 * i + b, LATW + R:, :] = zero_k
 
         if first:
             N = wk.shape[1]
@@ -259,9 +267,9 @@
     vm = pl.BlockSpec(memory_space=pltpu.VMEM)
     hbm = pl.BlockSpec(memory_space=pltpu.HBM)
     bf, f32 = jnp.bfloat16, jnp.float32
-    in_specs = [pl.BlockSpec(memory_space=pltpu.SMEM)] + ([hbm] * 3 if first else [vm] * 4)
+    in_specs = [hbm] * 3 if first else [hbm] + [vm] * 4
     keep = lambda xs, space: [pltpu.with_memory_space_constraint(x, space) for x in xs]
-    args = [pos, *keep(queries, pltpu.HBM if first else pltpu.VMEM)]
+    args = keep(queries, pltpu.HBM) if first else [*keep([pos], pltpu.HBM), *keep(queries, pltpu.VMEM)]
     if last:
         in_specs.append(hbm)
         args += keep([w_uv], pltpu.HBM)
@@ -300,6 +308,8 @@
         pltpu.SMEM((16,), jnp.int32),
         pltpu.SMEM((16,), jnp.int32),
     ]
+    if not first:
+        scratch += [pltpu.SMEM(pos.shape, jnp.int32), pltpu.SemaphoreType.DMA]
     if first:
         scratch += [
             pltpu.VMEM(qn.shape, bf),

time: 35.3 us -> 34.7 us (0.983)
  waiting for transfers between devices: 3.04 us -> 4.86 us
  Pallas kernels: 12.4 us -> 10.6 us
  local copies, waits for them, and re-layouts: 0.68 us -> 0 us
    ppermute x5, waiting for transfers between devices: 3.04 us -> 4.86 us  [per_device(): lax.ppermute(x, ('ctx', 'head'), pairs(n, heads, source))]
    pallas_call x3, Pallas kernels: 11.3 us -> 9.6 us  [phase(): pl.pallas_call(functools.partial(phase_kernel, first, last, offsets, wher...]
    unnamed x2 -> x0, local copies, waits for them, and re-layouts: 0.68 us -> none
  transfers between devices with their start and end apart: 5 -> 5, of which waited for: 2 -> 2; matrix products, arithmetic and copies ran while one was open for 0% -> 0% of each run, Pallas kernels for 14% -> 11%
where the time goes in v4:
time: 34.7 us; the launch traced here: 34.4 us
  starting transfers between devices  18.7 us (54%)
  Pallas kernels  10.6 us (31%)
  waiting for transfers between devices  4.86 us (14%)
    ppermute x5, starting transfers between devices, per_device(): lax.ppermute(x, ('ctx', 'head'), pairs(n, heads, source))  18.7 us
    pallas_call x3, Pallas kernels, phase(): pl.pallas_call(functools.partial(phase_kernel, first, last, offsets, wher...  9.6 us
    ppermute x5, waiting for transfers between devices, per_device(): lax.ppermute(x, ('ctx', 'head'), pairs(n, heads, source))  4.86 us
    pallas_call x1, Pallas kernels, pack(): pl.pallas_call(pack_kernel, out_shape=pltpu.VMEM((rows + k_rope_t.shape[0...  0.98 us
  transfers between devices with their start and end apart: 5, of which 2 were waited for; matrix products, arithmetic and copies ran while one was open for 0% of the time, Pallas kernels for 11%

profile of v4, /device:TPU:1, one launch (start us, length us, event | category | flops | bytes accessed | tf_op | source)
XLA Modules:
  0.0 34.4 jit_solution(769997754603871244)
XLA Ops:
  0.0 1.0 %pack.1.refs_3_ = bf16[288,512]{1,0:T(8,128)(2,1)S(1)} custom-call(bf16[256,512]{1,0:T(8,128)(2,1)} %c_h.1, bf16[64,256]{1,0:T(8,128)(2,1)} %bitcast.2), custom_call_target="tpu_custom_call" | custom-call | tf_op jit(solution)/shard_map/pack/pallas_call | solution.py:361
  1.0 4.0 %collective-permute-start = (bf16[288,512]{1,0:T(8,128)(2,1)S(1)}, bf16[288,512]{1,0:T(8,128)(2,1)S(1)}, u32[]{:S(2)}, u32[]{:S(2)}) collective-permute-start(bf16[288,512]{1,0:T(8,128)(2,1)S(1)} %pack.1.refs_3_), channel_id=1, source_target_pairs={{508,0},{509,1},{510,2},{511,3},{0,4},{1,5},{2,6},{3,7},{5,8},{4,9... | collective-permute-start | bytes 884744 | tf_op jit(solution)/shard_map/ppermute | solution.py:431
  5.0 1.3 %collective-permute-start.1 = (bf16[288,512]{1,0:T(8,128)(2,1)S(1)}, bf16[288,512]{1,0:T(8,128)(2,1)S(1)}, u32[]{:S(2)}, u32[]{:S(2)}) collective-permute-start(bf16[288,512]{1,0:T(8,128)(2,1)S(1)} %pack.1.refs_3_), channel_id=1, source_target_pairs={{4,0},{5,1},{6,2},{7,3},{9,4},{8,5},{11,6},{10,7},{12,8},{13,9},{1... | collective-permute-start | bytes 884744 | tf_op jit(solution)/shard_map/ppermute | solution.py:431
  6.3 3.6 %first.2 = (bf16[2,1024,640]{2,1,0:T(8,128)(2,1)S(1)}, f32[2,1024,128]{2,1,0:T(8,128)S(1)}, f32[2,1024,128]{2,1,0:T(8,128)S(1)}, f32[2,1024,512]{2,1,0:T(8,128)S(1)}, bf16[288,512]{1,0:T(8,128)(2,1)S(1)}) custom-call(bf16[256,8,128]{2,1,0:T(8,128)(2,1)} %refs_0_.4, bf16[8,64,256]{2,1,0:T(8,128)(2,1)} %bitcast.3, bf16[8,128,512]{2,1,0:T(8,128)(2,1)} %refs_2_.3, ...), custom_call_target="tpu_custom_call" | custom-call | flops 4000000000 | bytes 4194304 | tf_op jit(solution)/shard_map/first/pallas_call | solution.py:330
  9.9 8.9 %collective-permute-start.2 = (bf16[288,512]{1,0:T(8,128)(2,1)S(1)}, bf16[288,512]{1,0:T(8,128)(2,1)S(1)}, u32[]{:S(2)}, u32[]{:S(2)}) collective-permute-start(bf16[288,512]{1,0:T(8,128)(2,1)S(1)} %get-tuple-element.14.refs_3_.own), channel_id=1, source_target_pairs={{508,504},{509,505},{510,506},{511,507},{0,508},{1,509},{2,510},{3... | collective-permute-start | bytes 884744 | tf_op jit(solution)/shard_map/ppermute | solution.py:431
  18.9 4.0 %collective-permute-done.odd.refs_6_ = bf16[288,512]{1,0:T(8,128)(2,1)S(1)} collective-permute-done((bf16[288,512]{1,0:T(8,128)(2,1)S(1)}, bf16[288,512]{1,0:T(8,128)(2,1)S(1)}, u32[]{:S(2)}, u32[]{:S(2)}) %collective-permute-start) | collective-permute-done | bytes 294944 | tf_op jit(solution)/shard_map/ppermute | solution.py:431
  22.9 0.0 collective-permute-done.1.even.refs_7_
  22.9 3.8 %collective-permute-start.3 = (bf16[576,512]{1,0:T(8,128)(2,1)S(1)}, bf16[576,512]{1,0:T(8,128)(2,1)S(1)}, u32[]{:S(2)}, u32[]{:S(2)}) collective-permute-start(bf16[576,512]{1,0:T(8,128)(2,1)S(1)} %join_parity.1), channel_id=1, source_target_pairs={{2,0},{3,1},{0,2},{1,3},{6,4},{7,5},{4,6},{5,7},{10,8},{11,9},{8,1... | collective-permute-start | bytes 1769480 | tf_op jit(solution)/shard_map/ppermute | solution.py:431
  26.7 0.0 collective-permute-done.2.refs_0_.refs_8_
  26.7 0.7 %collective-permute-start.4 = (bf16[288,512]{1,0:T(8,128)(2,1)S(1)}, bf16[288,512]{1,0:T(8,128)(2,1)S(1)}, u32[]{:S(2)}, u32[]{:S(2)}) collective-permute-start(bf16[288,512]{1,0:T(8,128)(2,1)S(1)} %join.1), channel_id=1, source_target_pairs={{504,506},{505,507},{508,510},{509,511}} | collective-permute-start | bytes 884744 | tf_op jit(solution)/shard_map/ppermute | solution.py:431
  27.4 0.0 collective-permute-done.4.refs_10_
  27.4 0.9 %collective-permute-done.3.refs_9_ = bf16[576,512]{1,0:T(8,128)(2,1)S(1)} collective-permute-done((bf16[576,512]{1,0:T(8,128)(2,1)S(1)}, bf16[576,512]{1,0:T(8,128)(2,1)S(1)}, u32[]{:S(2)}, u32[]{:S(2)}) %collective-permute-start.3) | collective-permute-done | bytes 589856 | tf_op jit(solution)/shard_map/ppermute | solution.py:431
  28.3 5.9 %last.1 = bf16[256,8,128]{2,1,0:T(8,128)(2,1)} custom-call(s32[512]{0:T(512)} %refs_0_.5, bf16[2,1024,640]{2,1,0:T(8,128)(2,1)S(1)} %get-tuple-element.19.refs_1_, f32[2,1024,128]{2,1,0:T(8,128)S(1)} %get-tuple-element.20._.refs_1_.refs_2_, f32[2,1024,128]{2,1,0:T(8,128)S(1)} %get-tuple-element.21.refs_3_, f32[2,1024,512]{2,1,0:T(8,128)S(1)} %get-tuple-element.22.refs_4_, ...), custom_call_target="tpu_custom_call" | custom-call | flops 16000000000 | bytes 4194304 | tf_op jit(solution)/shard_map/last/pallas_call | solution.py:330
  (3 shorter events, 0.1 us)
Async XLA Ops:
  1.0 21.9 %collective-permute-start = (bf16[288,512]{1,0:T(8,128)(2,1)S(1)}, bf16[288,512]{1,0:T(8,128)(2,1)S(1)}, u32[]{:S(2)}, u32[]{:S(2)}) collective-permute-start(bf16[288,512]{1,0:T(8,128)(2,1)S(1)} %pack.1.refs_3_), channel_id=1, source_target_pairs={{508,0},{509,1},{510,2},{511,3},{0,4},{1,5},{2,6},{3,7},{5,8},{4,9... | collective-permute-start | bytes 884744 | tf_op jit(solution)/shard_map/ppermute | solution.py:431
  5.0 17.8 %collective-permute-start.1 = (bf16[288,512]{1,0:T(8,128)(2,1)S(1)}, bf16[288,512]{1,0:T(8,128)(2,1)S(1)}, u32[]{:S(2)}, u32[]{:S(2)}) collective-permute-start(bf16[288,512]{1,0:T(8,128)(2,1)S(1)} %pack.1.refs_3_), channel_id=1, source_target_pairs={{4,0},{5,1},{6,2},{7,3},{9,4},{8,5},{11,6},{10,7},{12,8},{13,9},{1... | collective-permute-start | bytes 884744 | tf_op jit(solution)/shard_map/ppermute | solution.py:431
  9.9 16.8 %collective-permute-start.2 = (bf16[288,512]{1,0:T(8,128)(2,1)S(1)}, bf16[288,512]{1,0:T(8,128)(2,1)S(1)}, u32[]{:S(2)}, u32[]{:S(2)}) collective-permute-start(bf16[288,512]{1,0:T(8,128)(2,1)S(1)} %get-tuple-element.14.refs_3_.own), channel_id=1, source_target_pairs={{508,504},{509,505},{510,506},{511,507},{0,508},{1,509},{2,510},{3... | collective-permute-start | bytes 884744 | tf_op jit(solution)/shard_map/ppermute | solution.py:431
  22.9 5.4 %collective-permute-start.3 = (bf16[576,512]{1,0:T(8,128)(2,1)S(1)}, bf16[576,512]{1,0:T(8,128)(2,1)S(1)}, u32[]{:S(2)}, u32[]{:S(2)}) collective-permute-start(bf16[576,512]{1,0:T(8,128)(2,1)S(1)} %join_parity.1), channel_id=1, source_target_pairs={{2,0},{3,1},{0,2},{1,3},{6,4},{7,5},{4,6},{5,7},{10,8},{11,9},{8,1... | collective-permute-start | bytes 1769480 | tf_op jit(solution)/shard_map/ppermute | solution.py:431
  26.7 0.7 %collective-permute-start.4 = (bf16[288,512]{1,0:T(8,128)(2,1)S(1)}, bf16[288,512]{1,0:T(8,128)(2,1)S(1)}, u32[]{:S(2)}, u32[]{:S(2)}) collective-permute-start(bf16[288,512]{1,0:T(8,128)(2,1)S(1)} %join.1), channel_id=1, source_target_pairs={{504,506},{505,507},{508,510},{509,511}} | collective-permute-start | bytes 884744 | tf_op jit(solution)/shard_map/ppermute | solution.py:431

commit v5 on v4

--- a/solution.py
+++ b/solution.py
@@ -12,6 +12,7 @@
 LOG2E = 1.4426950408889634
 CHUNK = 256
 AHEAD = 4
+PIECES = 4
 MIB = 1024 * 1024
 FL = 4e9
 
@@ -215,12 +216,15 @@
             for h in range(H):
                 o = os_[half, h * B:(h + 1) * B, :]
                 of[pl.ds(half * HB + h, B, stride=H), :] = jnp.dot(o, wv[h], preferred_element_type=jnp.float32)
-            rows = slice(half * HB, (half + 1) * HB)
-            ob[half * B:(half + 1) * B] = of[rows, :].reshape(B, H, of.shape[1]).astype(jnp.bfloat16)
-            out_copy(half).start()
-
-        def out_copy(half):
-            return pltpu.make_async_copy(ob.at[pl.ds(half * B, B)], out_h.at[pl.ds(half * B, B)], sem_o.at[half])
+            for k in range(PIECES):
+                rows = slice(half * HB + k * HB // PIECES, half * HB + (k + 1) * HB // PIECES)
+                toks = slice(half * B + k * B // PIECES, half * B + (k + 1) * B // PIECES)
+                ob[toks] = of[rows, :].reshape(B // PIECES, H, of.shape[1]).astype(jnp.bfloat16)
+                out_copy(half, k).start()
+
+        def out_copy(half, k):
+            toks = pl.ds(half * B + k * B // PIECES, B // PIECES)
+            return pltpu.make_async_copy(ob.at[toks], out_h.at[toks], sem_o.at[half * PIECES + k])
 
         if first:
             counts = [((2 + j) // 2, (2 * ns - j + 1) // 2) for j in range(ns)]
@@ -242,7 +246,8 @@
                     pl.when(items == n)(functools.partial(process, (half, n, lst, nb)))
         if last:
             for half in range(2):
-                out_copy(half).wait()
+                for k in range(PIECES):
+                    out_copy(half, k).wait()
 
     if when is None:
         run()
@@ -325,7 +330,7 @@
             pltpu.VMEM((T * H, w_uv.shape[2]), f32),
             pltpu.VMEM((T, H, w_uv.shape[2]), bf),
             pltpu.SemaphoreType.DMA,
-            pltpu.SemaphoreType.DMA((2,)),
+            pltpu.SemaphoreType.DMA((2 * PIECES,)),
         ]
     made = pl.pallas_call(
         functools.partial(phase_kernel, first, last, offsets, where, packed, when, again),
@@ -344,10 +349,15 @@
 def pack_kernel(c_h, r_h, out, sem):
     rows = c_h.shape[0]
     half = r_h.shape[0] // 2
+    piece = rows // 4
     copies = [
-        pltpu.make_async_copy(c_h, out.at[pl.ds(0, rows), :], sem.at[0]),
-        pltpu.make_async_copy(r_h.at[pl.ds(0, half), :], out.at[pl.ds(rows, half), pl.ds(0, rows)], sem.at[1]),
-        pltpu.make_async_copy(r_h.at[pl.ds(half, half), :], out.at[pl.ds(rows, half), pl.ds(rows, rows)], sem.at[2]),
+        pltpu.make_async_copy(
+            c_h.at[pl.ds(k * piece, piece), :], out.at[pl.ds(k * piece, piece), :], sem.at[2 + k]
+        )
+        for k in range(4)
+    ] + [
+        pltpu.make_async_copy(r_h.at[pl.ds(0, half), :], out.at[pl.ds(rows, half), pl.ds(0, rows)], sem.at[0]),
+        pltpu.make_async_copy(r_h.at[pl.ds(half, half), :], out.at[pl.ds(rows, half), pl.ds(rows, rows)], sem.at[1]),
     ]
     for copy in copies:
         copy.start()
@@ -363,7 +373,7 @@
         out_shape=pltpu.VMEM((rows + k_rope_t.shape[0] // 2, width), c_kv.dtype),
         in_specs=[hbm, hbm],
         out_specs=pl.BlockSpec(memory_space=pltpu.VMEM),
-        scratch_shapes=[pltpu.SemaphoreType.DMA((3,))],
+        scratch_shapes=[pltpu.SemaphoreType.DMA((6,))],
         compiler_params=pltpu.CompilerParams(vmem_limit_bytes=2 * MIB),
         name="pack",
     )(*[pltpu.with_memory_space_constraint(x, pltpu.HBM) for x in (c_kv, k_rope_t)])
@@ -421,7 +431,7 @@
             continue
         s %= n
         for h in range(heads):
-            hs = h if s // 4 == t // 4 or s // 16 != t // 16 else heads - 1 - h
+            hs = h if s // 4 == t // 4 or (s // 16 != t // 16 and not (abs(s - t) > n // 2 and t % 2)) else heads - 1 - h
             out.append((s * heads + hs, t * heads + h))
     return out
 

time: 34.7 us -> 34.3 us (0.988)
  starting transfers between devices: 18.7 us -> 18.3 us
  transfers between devices with their start and end apart: 5 -> 5, of which waited for: 2 -> 3; matrix products, arithmetic and copies ran while one was open for 0% -> 0% of each run, Pallas kernels for 11% -> 11%
where the time goes in v5:
time: 34.3 us; the launch traced here: 34.1 us
  starting transfers between devices  18.3 us (53%)
  Pallas kernels  10.6 us (31%)
  waiting for transfers between devices  4.86 us (14%)
    ppermute x5, starting transfers between devices, per_device(): lax.ppermute(x, ('ctx', 'head'), pairs(n, heads, source))  18.3 us
    pallas_call x3, Pallas kernels, phase(): pl.pallas_call(functools.partial(phase_kernel, first, last, offsets, wher...  9.58 us
    ppermute x5, waiting for transfers between devices, per_device(): lax.ppermute(x, ('ctx', 'head'), pairs(n, heads, source))  4.86 us
    pallas_call x1, Pallas kernels, pack(): pl.pallas_call(pack_kernel, out_shape=pltpu.VMEM((rows + k_rope_t.shape[0...  0.99 us
  transfers between devices with their start and end apart: 5, of which 3 were waited for; matrix products, arithmetic and copies ran while one was open for 0% of the time, Pallas kernels for 11%

profile of v5, /device:TPU:1, one launch (start us, length us, event | category | flops | bytes accessed | tf_op | source)
XLA Modules:
  0.0 34.1 jit_solution(5719581489743520426)
XLA Ops:
  0.0 1.0 %pack.1.refs_3_ = bf16[288,512]{1,0:T(8,128)(2,1)S(1)} custom-call(bf16[256,512]{1,0:T(8,128)(2,1)} %c_h.1, bf16[64,256]{1,0:T(8,128)(2,1)} %bitcast.2), custom_call_target="tpu_custom_call" | custom-call | tf_op jit(solution)/shard_map/pack/pallas_call | solution.py:371
  1.0 4.0 %collective-permute-start = (bf16[288,512]{1,0:T(8,128)(2,1)S(1)}, bf16[288,512]{1,0:T(8,128)(2,1)S(1)}, u32[]{:S(2)}, u32[]{:S(2)}) collective-permute-start(bf16[288,512]{1,0:T(8,128)(2,1)S(1)} %pack.1.refs_3_), channel_id=1, source_target_pairs={{508,0},{509,1},{511,2},{510,3},{0,4},{1,5},{2,6},{3,7},{5,8},{4,9... | collective-permute-start | bytes 884744 | tf_op jit(solution)/shard_map/ppermute | solution.py:441
  5.0 1.3 %collective-permute-start.1 = (bf16[288,512]{1,0:T(8,128)(2,1)S(1)}, bf16[288,512]{1,0:T(8,128)(2,1)S(1)}, u32[]{:S(2)}, u32[]{:S(2)}) collective-permute-start(bf16[288,512]{1,0:T(8,128)(2,1)S(1)} %pack.1.refs_3_), channel_id=1, source_target_pairs={{4,0},{5,1},{6,2},{7,3},{9,4},{8,5},{11,6},{10,7},{12,8},{13,9},{1... | collective-permute-start | bytes 884744 | tf_op jit(solution)/shard_map/ppermute | solution.py:441
  6.3 3.6 %first.2 = (bf16[2,1024,640]{2,1,0:T(8,128)(2,1)S(1)}, f32[2,1024,128]{2,1,0:T(8,128)S(1)}, f32[2,1024,128]{2,1,0:T(8,128)S(1)}, f32[2,1024,512]{2,1,0:T(8,128)S(1)}, bf16[288,512]{1,0:T(8,128)(2,1)S(1)}) custom-call(bf16[256,8,128]{2,1,0:T(8,128)(2,1)} %refs_0_.4, bf16[8,64,256]{2,1,0:T(8,128)(2,1)} %bitcast.3, bf16[8,128,512]{2,1,0:T(8,128)(2,1)} %refs_2_.3, ...), custom_call_target="tpu_custom_call" | custom-call | flops 4000000000 | bytes 4194304 | tf_op jit(solution)/shard_map/first/pallas_call | solution.py:335
  10.0 10.3 %collective-permute-start.2 = (bf16[288,512]{1,0:T(8,128)(2,1)S(1)}, bf16[288,512]{1,0:T(8,128)(2,1)S(1)}, u32[]{:S(2)}, u32[]{:S(2)}) collective-permute-start(bf16[288,512]{1,0:T(8,128)(2,1)S(1)} %get-tuple-element.14.refs_3_.own), channel_id=1, source_target_pairs={{508,504},{509,505},{510,506},{511,507},{0,508},{1,509},{3,510},{2... | collective-permute-start | bytes 884744 | tf_op jit(solution)/shard_map/ppermute | solution.py:441
  20.3 3.7 %collective-permute-done.odd.refs_6_ = bf16[288,512]{1,0:T(8,128)(2,1)S(1)} collective-permute-done((bf16[288,512]{1,0:T(8,128)(2,1)S(1)}, bf16[288,512]{1,0:T(8,128)(2,1)S(1)}, u32[]{:S(2)}, u32[]{:S(2)}) %collective-permute-start) | collective-permute-done | bytes 294944 | tf_op jit(solution)/shard_map/ppermute | solution.py:441
  24.0 0.0 collective-permute-done.1.even.refs_7_
  24.1 2.0 %collective-permute-start.3 = (bf16[576,512]{1,0:T(8,128)(2,1)S(1)}, bf16[576,512]{1,0:T(8,128)(2,1)S(1)}, u32[]{:S(2)}, u32[]{:S(2)}) collective-permute-start(bf16[576,512]{1,0:T(8,128)(2,1)S(1)} %join_parity.1), channel_id=1, source_target_pairs={{2,0},{3,1},{0,2},{1,3},{6,4},{7,5},{4,6},{5,7},{10,8},{11,9},{8,1... | collective-permute-start | bytes 1769480 | tf_op jit(solution)/shard_map/ppermute | solution.py:441
  26.1 0.7 %collective-permute-done.2.refs_0_.refs_8_ = bf16[288,512]{1,0:T(8,128)(2,1)S(1)} collective-permute-done((bf16[288,512]{1,0:T(8,128)(2,1)S(1)}, bf16[288,512]{1,0:T(8,128)(2,1)S(1)}, u32[]{:S(2)}, u32[]{:S(2)}) %collective-permute-start.2) | collective-permute-done | bytes 294944 | tf_op jit(solution)/shard_map/ppermute | solution.py:441
  26.8 0.7 %collective-permute-start.4 = (bf16[288,512]{1,0:T(8,128)(2,1)S(1)}, bf16[288,512]{1,0:T(8,128)(2,1)S(1)}, u32[]{:S(2)}, u32[]{:S(2)}) collective-permute-start(bf16[288,512]{1,0:T(8,128)(2,1)S(1)} %join.1), channel_id=1, source_target_pairs={{504,506},{505,507},{508,510},{509,511}} | collective-permute-start | bytes 884744 | tf_op jit(solution)/shard_map/ppermute | solution.py:441
  27.5 0.0 collective-permute-done.4.refs_10_
  27.5 0.5 %collective-permute-done.3.refs_9_ = bf16[576,512]{1,0:T(8,128)(2,1)S(1)} collective-permute-done((bf16[576,512]{1,0:T(8,128)(2,1)S(1)}, bf16[576,512]{1,0:T(8,128)(2,1)S(1)}, u32[]{:S(2)}, u32[]{:S(2)}) %collective-permute-start.3) | collective-permute-done | bytes 589856 | tf_op jit(solution)/shard_map/ppermute | solution.py:441
  28.0 5.9 %last.1 = bf16[256,8,128]{2,1,0:T(8,128)(2,1)} custom-call(s32[512]{0:T(512)} %refs_0_.5, bf16[2,1024,640]{2,1,0:T(8,128)(2,1)S(1)} %get-tuple-element.19.refs_1_, f32[2,1024,128]{2,1,0:T(8,128)S(1)} %get-tuple-element.20._.refs_1_.refs_2_, f32[2,1024,128]{2,1,0:T(8,128)S(1)} %get-tuple-element.21.refs_3_, f32[2,1024,512]{2,1,0:T(8,128)S(1)} %get-tuple-element.22.refs_4_, ...), custom_call_target="tpu_custom_call" | custom-call | flops 16000000000 | bytes 4194304 | tf_op jit(solution)/shard_map/last/pallas_call | solution.py:335
  (3 shorter events, 0.1 us)
Async XLA Ops:
  1.0 23.0 %collective-permute-start = (bf16[288,512]{1,0:T(8,128)(2,1)S(1)}, bf16[288,512]{1,0:T(8,128)(2,1)S(1)}, u32[]{:S(2)}, u32[]{:S(2)}) collective-permute-start(bf16[288,512]{1,0:T(8,128)(2,1)S(1)} %pack.1.refs_3_), channel_id=1, source_target_pairs={{508,0},{509,1},{511,2},{510,3},{0,4},{1,5},{2,6},{3,7},{5,8},{4,9... | collective-permute-start | bytes 884744 | tf_op jit(solution)/shard_map/ppermute | solution.py:441
  5.0 19.0 %collective-permute-start.1 = (bf16[288,512]{1,0:T(8,128)(2,1)S(1)}, bf16[288,512]{1,0:T(8,128)(2,1)S(1)}, u32[]{:S(2)}, u32[]{:S(2)}) collective-permute-start(bf16[288,512]{1,0:T(8,128)(2,1)S(1)} %pack.1.refs_3_), channel_id=1, source_target_pairs={{4,0},{5,1},{6,2},{7,3},{9,4},{8,5},{11,6},{10,7},{12,8},{13,9},{1... | collective-permute-start | bytes 884744 | tf_op jit(solution)/shard_map/ppermute | solution.py:441
  10.0 16.8 %collective-permute-start.2 = (bf16[288,512]{1,0:T(8,128)(2,1)S(1)}, bf16[288,512]{1,0:T(8,128)(2,1)S(1)}, u32[]{:S(2)}, u32[]{:S(2)}) collective-permute-start(bf16[288,512]{1,0:T(8,128)(2,1)S(1)} %get-tuple-element.14.refs_3_.own), channel_id=1, source_target_pairs={{508,504},{509,505},{510,506},{511,507},{0,508},{1,509},{3,510},{2... | collective-permute-start | bytes 884744 | tf_op jit(solution)/shard_map/ppermute | solution.py:441
  24.1 3.9 %collective-permute-start.3 = (bf16[576,512]{1,0:T(8,128)(2,1)S(1)}, bf16[576,512]{1,0:T(8,128)(2,1)S(1)}, u32[]{:S(2)}, u32[]{:S(2)}) collective-permute-start(bf16[576,512]{1,0:T(8,128)(2,1)S(1)} %join_parity.1), channel_id=1, source_target_pairs={{2,0},{3,1},{0,2},{1,3},{6,4},{7,5},{4,6},{5,7},{10,8},{11,9},{8,1... | collective-permute-start | bytes 1769480 | tf_op jit(solution)/shard_map/ppermute | solution.py:441
  26.8 0.7 %collective-permute-start.4 = (bf16[288,512]{1,0:T(8,128)(2,1)S(1)}, bf16[288,512]{1,0:T(8,128)(2,1)S(1)}, u32[]{:S(2)}, u32[]{:S(2)}) collective-permute-start(bf16[288,512]{1,0:T(8,128)(2,1)S(1)} %join.1), channel_id=1, source_target_pairs={{504,506},{505,507},{508,510},{509,511}} | collective-permute-start | bytes 884744 | tf_op jit(solution)/shard_map/ppermute | solution.py:441
